TPU v7x, 256 devices: a whole 4x4x8 slice. The times are simulated.
256 devices in a mesh: dp: 64 (over z, x, core), tensor: 4 (over y).
Axes of the slice: x: 4, y: 4, z: 8, core: 2. Of those that a mesh axis runs over, the one named last changes fastest.
Arguments:
- tokens: bfloat16 [8192, 4096], P(('dp', 'tensor')), may hold values from -6 to 6
- query_base_weight: bfloat16 [4096, 4096], P(None, 'tensor'), may hold values from -0.09375 to 0.09375
- adapter_down_weight: bfloat16 [64, 16, 4096], P('dp', None, 'tensor'), may hold values from -0.09375 to 0.09375
- adapter_up_weight: bfloat16 [64, 16, 4096], P('dp', None, 'tensor'), may hold values from -0.375 to 0.375
- upstream: bfloat16 [8192, 4096], P('dp', 'tensor'), may hold values from -6 to 6
- adapter_per_block: int32 [64, 1], P('dp'), may hold values from 0 to 63
- owner: int32 [64], replicated, may hold values from 0 to 63, each once
Outputs:
- mixed: bfloat16 [8192, 4096], P('dp', 'tensor')
- input_gradient: bfloat16 [8192, 4096], P(('dp', 'tensor'))
- down_gradient: float32 [64, 16, 4096], P('dp', None, 'tensor')
- up_gradient: float32 [64, 16, 4096], P('dp', None, 'tensor')
Inputs may be any that keep to these rules, and one draw needn't show every extreme that they name: `adapter_per_block`: every adapter has at least one block. `owner`: each slot is taken by exactly one adapter.
All inputs are finite; a program needn't handle non-finite values.
Results may differ from a plain program's by a relative error of at most 0.0032.
Values may be sent and summed in bfloat16 or wider, within the bound.
A program may use at most 128 MiB of HBM per device.

v0:
```python
import jax
import jax.numpy as jnp
from jax import lax
from jax.sharding import PartitionSpec as P

adapter_scale = 2.0


def per_device(
    tokens,
    query_base_weight,
    adapter_down_weight,
    adapter_up_weight,
    upstream,
    adapter_per_block,
    owner,
):
    tensor_index = lax.axis_index("tensor")
    col_width = query_base_weight.shape[1]
    blocks_here = adapter_per_block.shape[0]
    adapter_count = owner.shape[0]
    rank_width = adapter_down_weight.shape[1]
    gathered = lax.all_gather(tokens, "tensor", axis=0, tiled=True)
    block_len = gathered.shape[0] // blocks_here
    slot_indices = jnp.take(owner, adapter_per_block[:, 0])
    onehot = slot_indices[:, None] == jnp.arange(adapter_count, dtype=jnp.int32)[None, :]
    select = onehot.astype(jnp.bfloat16)
    down_all, up_all = (
        lax.all_gather(adapter_down_weight, "dp", axis=0, tiled=True),
        lax.all_gather(adapter_up_weight, "dp", axis=0, tiled=True),
    )
    down_pick = jnp.dot(
        select, down_all.reshape(adapter_count, -1), preferred_element_type=jnp.float32
    )
    up_pick = jnp.dot(select, up_all.reshape(adapter_count, -1), preferred_element_type=jnp.float32)
    down_chosen = down_pick.astype(jnp.bfloat16).reshape(blocks_here, rank_width, col_width)
    up_chosen = up_pick.astype(jnp.bfloat16).reshape(blocks_here, rank_width, col_width)
    owned_columns = lax.dynamic_slice_in_dim(gathered, tensor_index * col_width, col_width, 1)
    owned_columns = owned_columns.reshape(blocks_here, block_len, col_width)
    backward_blocks = upstream.reshape(blocks_here, block_len, col_width)
    reduced_portion = jnp.einsum(
        "mtn,myn->mty", owned_columns, down_chosen, preferred_element_type=jnp.float32
    )
    backward_portion = jnp.einsum(
        "mtn,myn->mty", backward_blocks, up_chosen, preferred_element_type=jnp.float32
    )
    reduced_hidden, reduced_backward = lax.psum((reduced_portion, backward_portion), "tensor")
    reduced_hidden = reduced_hidden.astype(jnp.bfloat16)
    reduced_backward = reduced_backward.astype(jnp.bfloat16)
    mixed = jnp.dot(gathered, query_base_weight, preferred_element_type=jnp.float32)
    mixed = mixed + adapter_scale * jnp.einsum(
        "xzv,xva->xza", reduced_hidden, up_chosen, preferred_element_type=jnp.float32
    ).reshape(-1, col_width)
    adapter_branch_term = adapter_scale * jnp.einsum(
        "xzv,xva->xza", reduced_backward, down_chosen, preferred_element_type=jnp.float32
    ).reshape(-1, col_width)
    partial_rows = lax.dot_general(
        upstream, query_base_weight, (((1,), (1,)), ((), ())), preferred_element_type=jnp.float32
    )
    current = lax.dynamic_slice_in_dim(partial_rows, tensor_index * col_width, col_width, 1)
    input_gradient = lax.psum_scatter(
        lax.dynamic_update_slice_in_dim(
            partial_rows, current + adapter_branch_term, tensor_index * col_width, 1
        ),
        "tensor",
        scatter_dimension=0,
        tiled=True,
    ).astype(jnp.bfloat16)
    down_contributions = adapter_scale * jnp.einsum(
        "phl,phj->plj", reduced_backward, owned_columns, preferred_element_type=jnp.float32
    )
    up_contributions = adapter_scale * jnp.einsum(
        "phl,phj->plj", reduced_hidden, backward_blocks, preferred_element_type=jnp.float32
    )
    spread = onehot.astype(jnp.float32).T
    dense_down = jnp.dot(
        spread, down_contributions.reshape(blocks_here, -1), precision=lax.Precision.HIGHEST
    )
    dense_up = jnp.dot(
        spread, up_contributions.reshape(blocks_here, -1), precision=lax.Precision.HIGHEST
    )
    down_gradient, up_gradient = (
        lax.psum_scatter(dense_down, "dp", scatter_dimension=0, tiled=True),
        lax.psum_scatter(dense_up, "dp", scatter_dimension=0, tiled=True),
    )
    down_gradient = down_gradient.reshape(adapter_down_weight.shape)
    up_gradient = up_gradient.reshape(adapter_up_weight.shape)
    return (mixed.astype(jnp.bfloat16), input_gradient, down_gradient, up_gradient)


def solution(mesh):
    return jax.shard_map(
        per_device,
        mesh=mesh,
        in_specs=(
            P(("dp", "tensor"), None),
            P(None, "tensor"),
            P("dp", None, "tensor"),
            P("dp", None, "tensor"),
            P("dp", "tensor"),
            P("dp", None),
            P(),
        ),
        out_specs=(
            P("dp", "tensor"),
            P(("dp", "tensor"), None),
            P("dp", None, "tensor"),
            P("dp", None, "tensor"),
        ),
        check_vma=False,
    )
```

profile of v0, /device:TPU:1, one launch (start us, length us, event | category | flops | bytes accessed | tf_op | source)
XLA Modules:
  0.0 464.5 jit_solution(12222215218337783466)
XLA Ops:
  7.2 0.7 all-gather.8.cloned.1.call-update
  8.0 0.7 all-gather.6.cloned.1.call-update
  8.7 0.7 all-gather.4.cloned.1.call-update
  10.1 1.2 dynamic-slice.2
  12.0 80.2 %all-gather.8.cloned.1.call-done = bf16[64,16,1024]{2,1,0:T(8,128)(2,1)} async-done(((bf16[1,16,1024]{2,1,0:T(8,128)(2,1)}), bf16[64,16,1024]{2,1,0:T(8,128)(2,1)}) %all-gather.8.cloned.1.call-update) | async-done | bytes 2097168 | tf_op jit(solution)/shard_map/all_gather | solution.py:30
  92.2 2.8 copy.12
  95.4 74.5 %all-gather.6.cloned.1.call-done = bf16[64,16,1024]{2,1,0:T(8,128)(2,1)} async-done(((bf16[1,16,1024]{2,1,0:T(8,128)(2,1)}), bf16[64,16,1024]{2,1,0:T(8,128)(2,1)}) %all-gather.6.cloned.1.call-update) | async-done | bytes 2097168 | tf_op jit(solution)/shard_map/all_gather | solution.py:29
  169.9 2.8 copy.11
  173.3 21.4 %all-gather.4.cloned.1.call-done = bf16[128,4096]{1,0:T(8,128)(2,1)} async-done(((bf16[32,4096]{1,0:T(8,128)(2,1)}), bf16[128,4096]{1,0:T(8,128)(2,1)}) %all-gather.4.cloned.1.call-update) | async-done | bytes 1048592 | tf_op jit(solution)/shard_map/all_gather | solution.py:23
  194.8 1.1 convolution_bitcast_fusion.1
  195.9 12.0 %all-reduce.3 = (bf16[1,128,16]{1,2,0:T(8,128)(2,1)S(1)}, bf16[1,128,16]{1,2,0:T(8,128)(2,1)S(1)}) all-reduce(f32[1,128,16]{1,2,0:T(8,128)S(1)} %convolution_bitcast_fusion.1, f32[1,128,16]{1,2,0:T(8,128)S(1)} %convolution_bitcast_fusion), channel_id=1, replica_groups=mesh['dp'=64,'tensor'=4] {'tensor'}, use_global_device_ids=true, to_apply=%region_0.1 | all-reduce | flops 4096 | bytes 24576 | tf_op jit(solution)/shard_map/psum | solution.py:47
  208.1 1.1 fusion.5
  209.2 4.1 broadcast_multiply_fusion
  213.4 6.2 %fusion.25 = f32[128,4096]{1,0:T(8,128)S(1)} fusion(bf16[128,1024]{1,0:T(8,128)(2,1)S(1)} %copy-done, bf16[4096,1024]{1,0:T(8,128)(2,1)} %param.8), kind=kOutput, calls=%fused_computation.37 | convolution fusion | flops 1073741824 | bytes 10747904 | tf_op jit(solution)/shard_map/dot_general | solution.py:57
  219.9 1.3 copy-done.1
  221.3 0.6 dynamic-slice.3
  221.9 4.7 %fusion.24 = f32[128,1024]{1,0:T(8,128)S(1)} fusion(bf16[128,4096]{1,0:T(8,128)(2,1)S(1)} %copy-done.2, bf16[4096,1024]{1,0:T(8,128)(2,1)} %param.8), kind=kOutput, calls=%fused_computation.36 | convolution fusion | flops 1073741824 | bytes 9961472 | tf_op jit(solution)/shard_map/dot_general | solution.py:50
  226.6 1.0 fusion.3
  227.5 193.6 %all-reduce.6.cloned.1.call-done = (f32[64,16384]{1,0:T(8,128)}, f32[64,16384]{1,0:T(8,128)}) async-done(((f32[64,16384]{1,0:T(8,128)}, f32[64,16384]{1,0:T(8,128)}), (f32[64,16384]{1,0:T(8,128)}, f32[64,16384]{1,0:T(8,128)})) %all-reduce.6.cloned.1.call-update) | async-done | bytes 8388624
  421.2 2.2 dynamic-slice_reduce_fusion
  423.4 0.6 reshape.129
  424.0 0.6 reshape.131
  424.6 31.6 %reduce-scatter.2.cloned.1.call-done = f32[32,4096]{1,0:T(8,128)} async-done(((f32[128,4096]{1,0:T(8,128)}), f32[32,4096]{1,0:T(8,128)}) %reduce-scatter.2.cloned.1.call-update) | async-done | bytes 524304 | tf_op jit(solution)/shard_map/reduce_scatter | solution.py:61
  456.2 1.8 convert_element_type.27
  (26 shorter events, 1.7 us)
Async XLA Ops:
  7.2 166.0 %copy-start = (bf16[128,1024]{1,0:T(8,128)(2,1)S(1)}, bf16[128,1024]{1,0:T(8,128)(2,1)}, u32[]{:S(2)}) copy-start(bf16[128,1024]{1,0:T(8,128)(2,1)} %param.11) | copy-start | bytes 786436
  7.2 85.0 %all-gather.8.cloned.1.call-start = ((), (), s32[]{:S(2)}) async-start(), calls=%async_computation.3 | async-start | bytes 2129920 | tf_op jit(solution)/shard_map/all_gather | solution.py:30
  7.9 162.0 %all-gather.6.cloned.1.call-start = ((), (), s32[]{:S(2)}) async-start(), calls=%async_computation.2 | async-start | bytes 2129920 | tf_op jit(solution)/shard_map/all_gather | solution.py:29
  8.7 186.1 %all-gather.4.cloned.1.call-start = ((), (), s32[]{:S(2)}) async-start(), calls=%async_computation.1 | async-start | bytes 1310720 | tf_op jit(solution)/shard_map/all_gather | solution.py:23
  9.4 411.8 %all-reduce.6.cloned.1.call-start = ((), (), s32[]{:S(2)}) async-start(), calls=%async_computation.5 | async-start | bytes 16777216
  213.3 7.9 %copy-start.3 = (u32[256]{0:T(256)S(1)}, u32[256]{0:T(256)}, u32[]{:S(2)}) copy-start(u32[256]{0:T(256)} %constant.56) | copy-start | bytes 3076
  213.3 242.9 %reduce-scatter.2.cloned.1.call-start = ((), (), s32[]{:S(2)}) async-start(), calls=%async_computation.4 | async-start | bytes 2621440 | tf_op jit(solution)/shard_map/reduce_scatter | solution.py:61
  219.6 2.2 copy-start.2
  219.9 1.3 copy-start.1
Sparse Core Ops, SparseCore 0:
  10.8 81.3 all-gather.7
  95.0 74.9 all-gather.5
  171.8 22.9 all-gather.3
  213.5 207.6 all-reduce.5
  423.7 32.4 reduce-scatter.1
where the time goes:
time: 465 us
  waiting for transfers between devices  403 us (87%)
  matrix products  15.5 us (3%)
  between operations  15.2 us (3%)
  local copies, waits for them, and re-layouts  12.3 us (3%)
  blocking collectives  12 us (3%)
  other arithmetic  5.89 us (1%)
    unnamed x6, waiting for transfers between devices  196 us
    all_gather x1, waiting for transfers between devices, per_device(): lax.all_gather(adapter_up_weight, 'dp', axis=0, tiled=True)  80.2 us
    all_gather x1, waiting for transfers between devices, per_device(): lax.all_gather(adapter_down_weight, 'dp', axis=0, tiled=True)  74.5 us
    reduce_scatter x1, waiting for transfers between devices, per_device(): lax.psum_scatter(lax.dynamic_update_slice_in_dim(partial_rows, current +...  31.6 us
    all_gather x1, waiting for transfers between devices, per_device(): gathered = lax.all_gather(tokens, 'tensor', axis=0, tiled=True)  21.4 us
    psum x1, blocking collectives, per_device(): lax.psum((reduced_portion, backward_portion), 'tensor')  12 us
    unnamed x14, local copies, waits for them, and re-layouts  9.76 us
  transfers between devices with their start and end apart: 5, of which 5 were waited for; matrix products, arithmetic and copies ran while one was open for 5% of the time, Pallas kernels for 0%

commit v1 on v0

v1 whole, which is shorter than its diff:
```python
import functools

import jax
import jax.numpy as jnp
from jax import lax
from jax.experimental import pallas as pl
from jax.experimental.pallas import tpu as pltpu
from jax.sharding import PartitionSpec as P

MESH = pl.DeviceIdType.MESH
SIDE = 8
RING = 4
RANK = 16
ITEM = 2 * RANK
LANE = 128
SLOTS = SIDE * SIDE
PARTS = SLOTS * 4

F32 = jnp.float32
BF16 = jnp.bfloat16


def dot(a, b):
    return jnp.dot(a, b, preferred_element_type=F32)


def dot_t(a, b):
    return lax.dot_general(a, b, (((1,), (1,)), ((), ())), preferred_element_type=F32)


def kernel(
    tokens, weight, down, up, upstream, adapter, owner,
    mixed_out, grad_out, down_out, up_out,
    w, tok, ups, part, send, relay_up, relay_dn, got_up, got_dn, mix, mix_b, rows_b,
    item, s1, r1, s2, r2, s3, r3, s4, r4, g1, h1, g2, h2, g3, h3, g4, h4,
    low_all, reorder, select, select_t, down_b, up_b,
    local_sem, out_sem, ag_s, ag_r, rs_s, rs_r, low_s, low_r, ph_s, ph_r,
):
    dp = lax.axis_index("dp")
    y = lax.axis_index("tensor")
    a, b = dp // SIDE, dp % SIDE
    rows = tokens.shape[0]
    cols = weight.shape[1]

    def ring(step):
        return (y + step) % RING

    def here(c):
        return pl.ds(pl.multiple_of(c * rows, rows), rows)

    def wide(c):
        return pl.ds(pl.multiple_of(c * cols, cols), cols)

    sent = []

    def push(src, dst, ssem, rsem, device):
        copy = pltpu.make_async_remote_copy(
            src_ref=src, dst_ref=dst, send_sem=ssem, recv_sem=rsem,
            device_id=device, device_id_type=MESH,
        )
        copy.start()
        sent.append(copy)
        return copy

    load_items = [
        pltpu.make_async_copy(down.at[0], item.at[pl.ds(0, RANK)], local_sem.at[0]),
        pltpu.make_async_copy(up.at[0], item.at[pl.ds(RANK, RANK)], local_sem.at[1]),
    ]
    order = (2, 1, 3, 0)
    load_tok = [
        pltpu.make_async_copy(
            tokens.at[:, wide(ring(k))], tok.at[ring(k), here(y)], local_sem.at[2 + k]
        )
        for k in range(RING)
    ]
    load_ups = pltpu.make_async_copy(upstream, ups, local_sem.at[6])
    load_w = [
        pltpu.make_async_copy(weight.at[wide(ring(k))], w.at[ring(k)], local_sem.at[7 + k])
        for k in range(RING)
    ]
    for copy in load_items:
        copy.start()
    for k in order:
        load_tok[k].start()
    load_ups.start()

    barrier = pltpu.get_barrier_semaphore()
    peers = [(dp, ring(k)) for k in range(1, RING)]
    peers += [(a * SIDE + (b + j) % SIDE, y) for j in range(1, SIDE)]
    peers += [((a + j) % SIDE * SIDE + b, y) for j in range(1, SIDE)]
    for device in peers:
        pl.semaphore_signal(barrier, inc=1, device_id=device, device_id_type=MESH)
    for k in (2, 3, 1, 0):
        load_w[k].start()

    row_id = lax.broadcasted_iota(jnp.int32, (PARTS, PARTS), 0)
    col_id = lax.broadcasted_iota(jnp.int32, (PARTS, PARTS), 1)
    flipped = (((row_id >> 2) & 7) << 5) | ((row_id >> 5) << 2) | (row_id & 3)
    reorder[...] = (col_id == flipped).astype(F32).astype(BF16)
    block_tag = jnp.full((RANK, LANE), adapter[0, 0], jnp.int32).astype(F32).astype(BF16)
    for copy in load_items:
        copy.wait()
    for k in range(SIDE):
        s1[k, 0:ITEM, :] = item[:, k * LANE:(k + 1) * LANE]
        s1[k, ITEM:, :] = block_tag
    r1[b] = s1[b]
    for k in order:
        load_tok[k].wait()

    pl.semaphore_wait(barrier, len(peers))

    up_dev, dn_dev = (dp, ring(1)), (dp, ring(3))

    def across(phase, src, dst):
        return [
            push(src.at[(b + j) % SIDE], dst.at[b], ph_s.at[phase, j], ph_r.at[phase, j],
                 (a * SIDE + (b + j) % SIDE, y))
            for j in range(1, SIDE)
        ]

    def along(phase, src, dst):
        return [
            push(src.at[(a + j) % SIDE], dst.at[a], ph_s.at[phase, j], ph_r.at[phase, j],
                 ((a + j) % SIDE * SIDE + b, y))
            for j in (4, 3, 5, 2, 6, 1, 7)
        ]

    def arrive(copies):
        for copy in copies:
            copy.wait_recv()

    def token_send(c, index, device):
        return push(tok.at[c, here(y)], tok.at[c, here(y)], ag_s.at[index], ag_r.at[index], device)

    def token_forward(c, owner_y, index, device):
        return push(tok.at[c, here(owner_y)], tok.at[c, here(owner_y)], ag_s.at[index], ag_r.at[index], device)

    ag_up = [token_send(ring(2), 0, up_dev)]
    ag_dn = [token_send(ring(3), 6, dn_dev)]
    first = across(0, s1, r1)
    ag_up.append(token_send(ring(1), 1, up_dev))
    ag_dn.append(token_send(ring(0), 7, dn_dev))
    ag_up.append(token_send(ring(3), 2, up_dev))
    ag_dn.append(token_send(ring(2), 8, dn_dev))
    ag_up.append(token_send(ring(0), 3, up_dev))
    ag_dn.append(token_send(ring(1), 9, dn_dev))

    def backward(k):
        c = ring(k)
        load_w[k].wait()
        if k == 2:
            load_ups.wait()
        part[c] = dot_t(ups[...], w[c])
        if k:
            send[c] = part[c].astype(BF16)

    backward(2)
    arrive(first)
    tags = r1[:, ITEM:, :].reshape(SIDE * RANK, LANE)
    tag_row = lax.broadcasted_iota(jnp.int32, (RANK, SIDE * RANK), 0)
    tag_col = lax.broadcasted_iota(jnp.int32, (RANK, SIDE * RANK), 1)
    pick = ((tag_col == (tag_row << 4)) & (tag_row < SIDE)).astype(F32).astype(BF16)
    row_tags = dot(pick, tags).astype(BF16)
    pieces = dot(reorder[...], r1[:, 0:ITEM, :].reshape(PARTS, LANE)).astype(BF16)
    s2[:, 0:ITEM, :] = pieces.reshape(SIDE, ITEM, LANE)
    for k in range(SIDE):
        s2[k, ITEM:, :] = row_tags
    r2[a] = s2[a]
    second = along(1, s2, r2)

    ag_up[0].wait_recv()
    ag_up.append(token_forward(ring(1), ring(3), 4, up_dev))
    ag_dn[0].wait_recv()
    ag_dn.append(token_forward(ring(0), ring(1), 10, dn_dev))
    backward(3)

    arrive(second)
    tags = r2[:, ITEM:, :].reshape(SIDE * RANK, LANE)
    part_row = lax.broadcasted_iota(jnp.int32, (PARTS, SIDE * RANK), 0)
    tag_col = lax.broadcasted_iota(jnp.int32, (PARTS, SIDE * RANK), 1)
    pick = (tag_col == (((part_row >> 5) << 4) | ((part_row >> 2) & 7))).astype(F32).astype(BF16)
    adapter_of = dot(pick, tags)[:, 0:SLOTS].astype(jnp.int32)
    lane = lax.broadcasted_iota(jnp.int32, (PARTS, SLOTS), 1)
    uses = (adapter_of == lane).astype(F32).astype(BF16)
    slot_row = lax.broadcasted_iota(jnp.int32, (PARTS, SLOTS), 0) >> 2
    owns = (owner[...] == slot_row).astype(F32).astype(BF16)
    same_part = ((row_id ^ col_id) & 3) == 0
    select[...] = jnp.where(same_part, dot_t(uses, owns), 0.0).astype(BF16)
    chosen_parts = dot(select[...], r2[:, 0:ITEM, :].reshape(PARTS, LANE)).astype(BF16)
    s3[...] = chosen_parts.reshape(SIDE, ITEM, LANE)
    r3[a] = s3[a]
    third = along(2, s3, r3)
    select_t[...] = jnp.where(same_part, dot_t(owns, uses), 0.0).astype(BF16)

    ag_up[1].wait_recv()
    ag_up.append(token_forward(ring(0), ring(3), 5, up_dev))
    ag_dn[1].wait_recv()
    ag_dn.append(token_forward(ring(1), ring(1), 11, dn_dev))
    backward(1)

    arrive(third)
    s4[...] = dot(reorder[...], r3[...].reshape(PARTS, LANE)).astype(BF16).reshape(SIDE, ITEM, LANE)
    r4[b] = s4[b]
    fourth = across(3, s4, r4)
    backward(0)

    def rows_send(c, to, dst, index, device):
        return push(send.at[c, here(to)], dst, rs_s.at[index], rs_r.at[index], device)

    far_up = [
        rows_send(ring(2), ring(2), relay_up.at[0], 0, up_dev),
        rows_send(ring(3), ring(2), relay_up.at[1], 1, up_dev),
    ]
    far_dn = [rows_send(ring(1), ring(2), relay_dn.at[0], 6, dn_dev)]
    near_up = [rows_send(ring(3), ring(1), got_up.at[ring(3)], 2, up_dev)]
    near_dn = [rows_send(ring(3), ring(3), got_dn.at[ring(3)], 8, dn_dev)]

    arrive(fourth)
    down_here = jnp.concatenate([r4[k, 0:RANK, :] for k in range(SIDE)], axis=1)
    up_here = jnp.concatenate([r4[k, RANK:, :] for k in range(SIDE)], axis=1)
    low_all[y, RANK:, :] = dot_t(up_here, ups[...])
    for copy in (ag_up[4],):
        copy.wait_recv()
    low_all[y, 0:RANK, :] = dot_t(down_here, tok[y])
    lows = [
        push(low_all.at[y], low_all.at[y], low_s.at[k - 1], low_r.at[k - 1], (dp, ring(k)))
        for k in range(1, RING)
    ]

    def relayed(c, to, relay, dst, index, device):
        send[c, here(to), :] = (part[c, here(to), :] + relay[...].astype(F32)).astype(BF16)
        return rows_send(c, to, dst, index, device)

    far_up[0].wait_recv()
    near_up.append(relayed(ring(1), ring(1), relay_up.at[0], got_up.at[ring(1)], 3, up_dev))
    far_dn[0].wait_recv()
    near_dn.append(relayed(ring(2), ring(3), relay_dn.at[0], got_dn.at[ring(2)], 9, dn_dev))
    far_up[1].wait_recv()
    near_up.append(relayed(ring(2), ring(1), relay_up.at[1], got_up.at[ring(2)], 4, up_dev))

    mix[...] = dot(tok[y], w[y])

    arrive(lows)
    total = low_all[0] + low_all[1] + low_all[2] + low_all[3]
    low_t = total[0:RANK].astype(BF16)
    back_t = total[RANK:].astype(BF16)
    flat = total.T
    low = flat[:, 0:RANK].astype(BF16)
    back = flat[:, RANK:].astype(BF16)

    down_term = (2.0 * dot(back_t, tok[y])).astype(BF16)
    up_term = (2.0 * dot(low_t, ups[...])).astype(BF16)
    for k in range(SIDE):
        g1[k, 0:RANK, :] = down_term[:, k * LANE:(k + 1) * LANE]
        g1[k, RANK:, :] = up_term[:, k * LANE:(k + 1) * LANE]
    h1[b] = g1[b]
    first = across(4, g1, h1)

    part[y] = part[y] + 2.0 * dot(back, down_here)
    send[y] = part[y].astype(BF16)
    far_dn.append(rows_send(y, ring(2), relay_dn.at[1], 7, dn_dev))
    near_up.append(rows_send(y, ring(1), got_up.at[y], 5, up_dev))
    near_dn.append(rows_send(y, ring(3), got_dn.at[y], 10, dn_dev))
    mix[...] += 2.0 * dot(low, up_here)

    arrive(first)
    g2[...] = dot(reorder[...], h1[...].reshape(PARTS, LANE)).astype(BF16).reshape(SIDE, ITEM, LANE)
    h2[a] = g2[a]
    second = along(5, g2, h2)

    ag_up[2].wait_recv()
    ag_up[3].wait_recv()
    ag_up[5].wait_recv()
    ag_dn[2].wait_recv()
    ag_dn[3].wait_recv()
    ag_dn[4].wait_recv()
    ag_dn[5].wait_recv()
    mix[...] += dot(tok[ring(1)], w[ring(1)])

    arrive(second)
    owned = dot(select_t[...], h2[...].reshape(PARTS, LANE)).astype(BF16)
    g3[...] = owned.reshape(SIDE, ITEM, LANE)
    h3[a] = g3[a]
    third = along(6, g3, h3)

    far_dn[1].wait_recv()
    near_dn.append(relayed(ring(1), ring(3), relay_dn.at[1], got_dn.at[ring(1)], 11, dn_dev))

    mix[...] += dot(tok[ring(3)], w[ring(3)])

    arrive(third)
    g4[...] = dot(reorder[...], h3[...].reshape(PARTS, LANE)).astype(BF16).reshape(SIDE, ITEM, LANE)
    h4[b] = g4[b]
    fourth = across(7, g4, h4)

    mix_b[...] = (mix[...] + dot(tok[ring(2)], w[ring(2)])).astype(BF16)
    outs = [pltpu.make_async_copy(mix_b, mixed_out, out_sem.at[0])]
    outs[0].start()

    arrive(fourth)
    for k in range(SIDE):
        down_b[:, k * LANE:(k + 1) * LANE] = h4[k, 0:RANK, :].astype(F32)
        up_b[:, k * LANE:(k + 1) * LANE] = h4[k, RANK:, :].astype(F32)
    outs.append(pltpu.make_async_copy(down_b, down_out.at[0], out_sem.at[1]))
    outs[-1].start()
    outs.append(pltpu.make_async_copy(up_b, up_out.at[0], out_sem.at[2]))
    outs[-1].start()

    arrive(near_up)
    arrive(near_dn)
    for k in range(RING):
        c = ring(k)
        rows_b[c] = (
            part[c, here(y), :] + got_up[c].astype(F32) + got_dn[c].astype(F32)
        ).astype(BF16)
        outs.append(pltpu.make_async_copy(rows_b.at[c], grad_out.at[:, wide(c)], out_sem.at[3 + k]))
        outs[-1].start()
    for copy in sent:
        copy.wait_send()
    for copy in outs:
        copy.wait()


def per_device(tokens, weight, down, up, upstream, adapter, owner):
    rows, width = tokens.shape
    block, cols = upstream.shape
    any_spec = pl.BlockSpec(memory_space=pl.ANY)
    small = lambda: pltpu.VMEM((SIDE, ITEM, LANE), BF16)
    tagged = lambda: pltpu.VMEM((SIDE, ITEM + RANK, LANE), BF16)
    dma = lambda *shape: pltpu.SemaphoreType.DMA(shape)
    scratch = [
        pltpu.VMEM((RING, cols, cols), BF16),
        pltpu.VMEM((RING, block, cols), BF16),
        pltpu.VMEM((block, cols), BF16),
        pltpu.VMEM((RING, block, cols), F32),
        pltpu.VMEM((RING, block, cols), BF16),
        pltpu.VMEM((2, rows, cols), BF16),
        pltpu.VMEM((2, rows, cols), BF16),
        pltpu.VMEM((RING, rows, cols), BF16),
        pltpu.VMEM((RING, rows, cols), BF16),
        pltpu.VMEM((block, cols), F32),
        pltpu.VMEM((block, cols), BF16),
        pltpu.VMEM((RING, rows, cols), BF16),
        pltpu.VMEM((ITEM, cols), BF16),
        tagged(), tagged(), tagged(), tagged(),
        small(), small(), small(), small(),
        small(), small(), small(), small(), small(), small(), small(), small(),
        pltpu.VMEM((RING, ITEM, block), F32),
        pltpu.VMEM((PARTS, PARTS), BF16),
        pltpu.VMEM((PARTS, PARTS), BF16),
        pltpu.VMEM((PARTS, PARTS), BF16),
        pltpu.VMEM((RANK, cols), F32),
        pltpu.VMEM((RANK, cols), F32),
        dma(11), dma(7), dma(12), dma(12), dma(12), dma(12), dma(3), dma(3),
        dma(8, SIDE), dma(8, SIDE),
    ]
    return pl.pallas_call(
        kernel,
        out_shape=(
            jax.ShapeDtypeStruct((block, cols), BF16),
            jax.ShapeDtypeStruct((rows, width), BF16),
            jax.ShapeDtypeStruct(down.shape, F32),
            jax.ShapeDtypeStruct(up.shape, F32),
        ),
        in_specs=[any_spec] * 5
        + [pl.BlockSpec(memory_space=pltpu.SMEM), pl.BlockSpec(memory_space=pltpu.VMEM)],
        out_specs=(any_spec,) * 4,
        scratch_shapes=scratch,
        compiler_params=pltpu.CompilerParams(
            collective_id=0, has_side_effects=True, vmem_limit_bytes=56 * 1024 * 1024
        ),
        cost_estimate=pl.CostEstimate(
            flops=4 * block * width * cols, bytes_accessed=12 * 1024 * 1024, transcendentals=0
        ),
    )(tokens, weight, down, up, upstream, adapter, owner.reshape(1, -1))


def solution(mesh):
    return jax.shard_map(
        per_device,
        mesh=mesh,
        in_specs=(
            P(("dp", "tensor"), None),
            P(None, "tensor"),
            P("dp", None, "tensor"),
            P("dp", None, "tensor"),
            P("dp", "tensor"),
            P("dp", None),
            P(),
        ),
        out_specs=(
            P("dp", "tensor"),
            P(("dp", "tensor"), None),
            P("dp", None, "tensor"),
            P("dp", None, "tensor"),
        ),
        check_vma=False,
    )
```

time: 465 us -> 61.1 us (0.13)
  waiting for transfers between devices: 403 us -> 0 us
  Pallas kernels: 0 us -> 53.3 us
  matrix products: 15.5 us -> 0 us
  between operations: 15.2 us -> 1.29 us
  blocking collectives: 12 us -> 0 us
  local copies, waits for them, and re-layouts: 12.3 us -> 6.28 us
  other arithmetic: 5.89 us -> 0 us
    unnamed x6 -> x0, waiting for transfers between devices: 196 us -> none
    all_gather x3 -> x0, waiting for transfers between devices: 176 us -> none  [the longest x1 80.2 us: per_device(): lax.all_gather(adapter_up_weight, 'dp', axis=0, tiled=True)]
    pallas_call x0 -> x1, Pallas kernels: none -> 53.3 us  [per_device(): pl.pallas_call(kernel, out_shape=(jax.ShapeDtypeStruct((block, cols), BF1...]
    reduce_scatter x1 -> x0, waiting for transfers between devices: 31.6 us -> none  [per_device(): lax.psum_scatter(lax.dynamic_update_slice_in_dim(partial_rows, current +...]
    dot_general x10 -> x0, matrix products: 15.5 us -> none  [the longest x1 6.24 us: per_device(): lax.dot_general(upstream, query_base_weight, (((1,), (1,)), ((), ())), pr...]
    psum x1 -> x0, blocking collectives: 12 us -> none  [per_device(): lax.psum((reduced_portion, backward_portion), 'tensor')]
    unnamed x14 -> x4, local copies, waits for them, and re-layouts: 9.76 us -> 6.28 us
  transfers between devices with their start and end apart: 5 -> 0, of which waited for: 5 -> 0; matrix products, arithmetic and copies ran while one was open for 5% -> 0% of each run, Pallas kernels for 0% -> 0%
where the time goes in v1:
time: 61.1 us; the launch traced here: 60.9 us
  Pallas kernels  53.3 us (87%)
  local copies, waits for them, and re-layouts  6.28 us (10%)
  between operations  1.29 us (2%)
    pallas_call x1, Pallas kernels, per_device(): pl.pallas_call(kernel, out_shape=(jax.ShapeDtypeStruct((block, cols), BF1...  53.3 us
    unnamed x4, local copies, waits for them, and re-layouts  6.28 us

profile of v1, /device:TPU:1, one launch (start us, length us, event | category | flops | bytes accessed | tf_op | source)
XLA Modules:
  0.0 60.9 jit_solution(11585919331207590610)
XLA Ops:
  1.3 53.3 %shard_map.102 = (bf16[128,1024]{1,0:T(8,128)(2,1)}, bf16[32,4096]{1,0:T(8,128)(2,1)}, f32[1,16,1024]{2,1,0:T(8,128)}, f32[1,16,1024]{2,1,0:T(8,128)}) custom-call(bf16[32,4096]{1,0:T(8,128)(2,1)} %tokens.1, bf16[4096,1024]{1,0:T(8,128)(2,1)} %weight.1, bf16[1,16,1024]{2,1,0:T(8,128)(2,1)} %down.1, bf16[1,16,1024]{2,1,0:T(8,128)(2,1)} %up.1, ...), custom_call_target="tpu_custom_call" | custom-call | flops 2147483648 | bytes 12582912 | tf_op jit(solution)/shard_map/pallas_call | solution.py:357
  54.6 1.7 %copy.16 = bf16[128,1024]{1,0:T(8,128)(2,1)} copy(bf16[128,1024]{1,0:T(8,128)(2,1)} %get-tuple-element.8) | data formatting | bytes 524288
  56.3 1.7 %copy.17 = bf16[32,4096]{1,0:T(8,128)(2,1)} copy(bf16[32,4096]{1,0:T(8,128)(2,1)} %get-tuple-element.9) | data formatting | bytes 524288
  57.9 1.5 %copy.18 = f32[1,16,1024]{2,1,0:T(8,128)} copy(f32[1,16,1024]{2,1,0:T(8,128)} %get-tuple-element.10) | data formatting | bytes 131072
  59.4 1.5 %copy.19 = f32[1,16,1024]{2,1,0:T(8,128)} copy(f32[1,16,1024]{2,1,0:T(8,128)} %get-tuple-element.11) | data formatting | bytes 131072

commit v2 on v1

v2 whole, which is shorter than its diff:
```python
import jax
import jax.numpy as jnp
from jax import lax
from jax.experimental import pallas as pl
from jax.experimental.pallas import tpu as pltpu
from jax.sharding import PartitionSpec as P

MESH = pl.DeviceIdType.MESH
DEEP = 8
WIDE = 4
CHIPS = DEEP * WIDE
RING = 4
RANK = 16
ITEM = 2 * RANK
TILE = 8
TAGGED = 2 * TILE
LANE = 128
FAR_FIRST = [
    (dz, dx) for dz in (4, 3, 5, 2, 6, 1, 7, 0) for dx in (2, 1, 3, 0) if dz or dx
]

F32 = jnp.float32
BF16 = jnp.bfloat16


def dot(a, b):
    return jnp.dot(a, b, preferred_element_type=F32)


def dot_t(a, b):
    return lax.dot_general(a, b, (((1,), (1,)), ((), ())), preferred_element_type=F32)


def one_hot(condition):
    return condition.astype(F32).astype(BF16)


def ids(rows, cols, dim):
    return lax.broadcasted_iota(jnp.int32, (rows, cols), dim)


def kernel(
    tokens, weight, down, up, upstream, adapter, owner,
    mixed_out, grad_out, down_out, up_out,
    w, tok, ups, part, send, relay_up, relay_dn, got_up, got_dn, mix,
    item, s1, r1, s3, r3, g1, h1, g3, h3, low_all, back_a, back_b,
    local_sem, ag_s, ag_r, rs_s, rs_r, low_s, low_r, ph_s, ph_r,
):
    dp = lax.axis_index("dp")
    y = lax.axis_index("tensor")
    chip, core = dp // 2, dp % 2
    other = 1 - core
    z, x = chip // WIDE, chip % WIDE
    z_at = [lax.rem(z + j, DEEP) for j in range(DEEP)]
    x_at = [lax.rem(x + j, WIDE) for j in range(WIDE)]
    rows = tokens.shape[0]
    cols = weight.shape[1]
    ring_at = [lax.rem(y + j, RING) for j in range(RING)]
    sibling = (chip * 2 + other, y)

    def ring(step):
        return ring_at[step]

    def here(c):
        return pl.ds(pl.multiple_of(c * rows, rows), rows)

    def wide(c):
        return pl.ds(pl.multiple_of(c * cols, cols), cols)

    sent = []

    def push(src, dst, ssem, rsem, device):
        copy = pltpu.make_async_remote_copy(
            src_ref=src, dst_ref=dst, send_sem=ssem, recv_sem=rsem,
            device_id=device, device_id_type=MESH,
        )
        copy.start()
        sent.append(copy)
        return copy

    load_items = [
        pltpu.make_async_copy(down.at[0], item.at[pl.ds(0, RANK)], local_sem.at[0]),
        pltpu.make_async_copy(up.at[0], item.at[pl.ds(RANK, RANK)], local_sem.at[1]),
    ]
    order = (2, 1, 3, 0)
    load_tok = [
        pltpu.make_async_copy(
            tokens.at[:, wide(ring(k))], tok.at[ring(k), here(y)], local_sem.at[2 + k]
        )
        for k in range(RING)
    ]
    load_ups = pltpu.make_async_copy(upstream, ups, local_sem.at[6])
    load_w = [
        pltpu.make_async_copy(weight.at[wide(ring(k))], w.at[ring(k)], local_sem.at[7 + k])
        for k in range(RING)
    ]
    for copy in load_items:
        copy.start()

    barrier = pltpu.get_barrier_semaphore()

    def chip_at(dz, dx):
        return z_at[dz] * WIDE + x_at[dx]

    peers = [(chip_at(dz, dx) * 2 + core, y) for dz, dx in FAR_FIRST]
    peers += [(dp, ring(k)) for k in (2, 1, 3)] + [sibling]
    for device in peers:
        pl.semaphore_signal(barrier, inc=1, device_id=device, device_id_type=MESH)
    for k in order:
        load_tok[k].start()
    load_ups.start()
    for k in (2, 3, 1, 0):
        load_w[k].start()

    tag = jnp.full((TILE, LANE), adapter[0, 0], jnp.int32).astype(F32)
    for copy in load_items:
        copy.wait()
    for t in range(CHIPS):
        down_rows = (t % 4) * TILE
        lanes = (t // 4) * LANE
        if t % 2 == 0:
            pair = item[down_rows:down_rows + 2 * TILE, lanes:lanes + LANE].astype(F32)
        half = pair[(t % 2) * TILE:(t % 2 + 1) * TILE]
        s1[t] = jnp.concatenate([half, tag], axis=0).astype(BF16)
    for k in order:
        load_tok[k].wait()

    pl.semaphore_wait(barrier, len(peers))

    up_dev, dn_dev = (dp, ring(1)), (dp, ring(3))

    def spread(phase, src, dst, mine):
        for dz, dx in FAR_FIRST:
            to = chip_at(dz, dx)
            pltpu.make_async_remote_copy(
                src_ref=src.at[to], dst_ref=dst(chip), send_sem=ph_s.at[phase],
                recv_sem=ph_r.at[phase], device_id=(to * 2 + core, y), device_id_type=MESH,
            ).start()
        pltpu.make_async_copy(src.at[chip], dst(chip), ph_r.at[phase]).start()
        return pltpu.make_async_copy(mine, mine, ph_r.at[phase])

    def drain(phase, src):
        others = src.at[pl.ds(0, CHIPS - 1)]
        pltpu.make_async_copy(others, others, ph_s.at[phase]).wait()

    def arrive(copies):
        for copy in copies:
            copy.wait_recv()

    def token_send(c, owner_y, index, device):
        return push(tok.at[c, here(owner_y)], tok.at[c, here(owner_y)], ag_s.at[index], ag_r.at[index], device)

    first = spread(0, s1, lambda i: r1.at[core, i], r1.at[core])
    ag_up = [token_send(ring(2), y, 0, up_dev)]
    ag_dn = [token_send(ring(3), y, 6, dn_dev)]
    ag_up.append(token_send(ring(1), y, 1, up_dev))
    ag_dn.append(token_send(ring(0), y, 7, dn_dev))
    ag_up.append(token_send(ring(3), y, 2, up_dev))
    ag_dn.append(token_send(ring(2), y, 8, dn_dev))
    ag_up.append(token_send(ring(0), y, 3, up_dev))
    ag_dn.append(token_send(ring(1), y, 9, dn_dev))

    def backward(k):
        c = ring(k)
        load_w[k].wait()
        if k == 2:
            load_ups.wait()
        part[c] = dot_t(ups[...], w[c])
        if k:
            send[c] = part[c].astype(BF16)

    adapters = owner.shape[1]
    out_rows, tagged_rows = CHIPS * TILE, CHIPS * TAGGED
    pick = one_hot(
        ids(out_rows, tagged_rows, 1) == ((ids(out_rows, tagged_rows, 0) >> 3) << 4) + TILE
    )

    def users(got):
        tags = dot(pick, got).astype(jnp.int32)[:, 0:adapters]
        return one_hot(tags == ids(out_rows, adapters, 1))

    def owners(n_rows, shift, which):
        return one_hot(owner[...] == (ids(n_rows, adapters, 0) >> shift) * 2 + which)

    slots_a = owners(tagged_rows, 4, core)
    slots_b = owners(tagged_rows, 4, other)
    same = (ids(out_rows, tagged_rows, 0) & 7) == (ids(out_rows, tagged_rows, 1) & 15)
    same_back = (ids(out_rows, out_rows, 0) & 7) == (ids(out_rows, out_rows, 1) & 7)

    backward(2)
    backward(3)
    ag_up[0].wait_recv()
    ag_up.append(token_send(ring(1), ring(3), 4, up_dev))
    ag_dn[0].wait_recv()
    ag_dn.append(token_send(ring(0), ring(1), 10, dn_dev))

    first.wait()
    swap = push(r1.at[core], r1.at[core], ph_s.at[1], ph_r.at[1], sibling)
    got = r1[core].reshape(tagged_rows, LANE)
    users_a = users(got)
    take_a = jnp.where(same, dot_t(users_a, slots_a), 0.0).astype(BF16)
    take_b = jnp.where(same, dot_t(users_a, slots_b), 0.0).astype(BF16)
    chosen = dot(take_a, got)
    swap.wait_recv()
    got = r1[other].reshape(tagged_rows, LANE)
    s3[...] = (chosen + dot(take_b, got)).reshape(CHIPS, TILE, LANE)
    second = spread(2, s3, lambda i: r3.at[i], r3)

    ag_up[1].wait_recv()
    ag_up.append(token_send(ring(0), ring(3), 5, up_dev))
    ag_dn[1].wait_recv()
    ag_dn.append(token_send(ring(1), ring(1), 11, dn_dev))

    slots_back = owners(out_rows, 3, core)
    back_a[...] = jnp.where(same_back, dot_t(slots_back, users_a), 0.0).astype(BF16)
    back_b[...] = jnp.where(same_back, dot_t(slots_back, users(got)), 0.0).astype(BF16)

    backward(1)

    def rows_send(c, to, dst, index, device):
        return push(send.at[c, here(to)], dst, rs_s.at[index], rs_r.at[index], device)

    far_up = [
        rows_send(ring(2), ring(2), relay_up.at[0], 0, up_dev),
        rows_send(ring(3), ring(2), relay_up.at[1], 1, up_dev),
    ]
    far_dn = [rows_send(ring(1), ring(2), relay_dn.at[0], 6, dn_dev)]
    near_up = [rows_send(ring(3), ring(1), got_up.at[ring(3)], 2, up_dev)]
    near_dn = [rows_send(ring(3), ring(3), got_dn.at[ring(3)], 8, dn_dev)]

    backward(0)
    ag_up[4].wait_recv()
    mix[...] = dot(tok[y], w[y])

    second.wait()

    def half_item(base):
        return jnp.concatenate(
            [
                jnp.concatenate([r3[lane * 4 + base], r3[lane * 4 + base + 1]], axis=0)
                for lane in range(cols // LANE)
            ],
            axis=1,
        ).astype(BF16)

    down_here, up_here = half_item(0), half_item(2)
    low_all[y, RANK:, :] = dot_t(up_here, ups[...])
    low_all[y, 0:RANK, :] = dot_t(down_here, tok[y])
    lows = [
        push(low_all.at[y], low_all.at[y], low_s.at[k - 1], low_r.at[k - 1], (dp, ring(k)))
        for k in (2, 1, 3)
    ]

    def relayed(c, to, relay, dst, index, device):
        send[c, here(to), :] = (part[c, here(to), :] + relay[...].astype(F32)).astype(BF16)
        return rows_send(c, to, dst, index, device)

    far_up[0].wait_recv()
    near_up.append(relayed(ring(1), ring(1), relay_up.at[0], got_up.at[ring(1)], 3, up_dev))
    far_dn[0].wait_recv()
    near_dn.append(relayed(ring(2), ring(3), relay_dn.at[0], got_dn.at[ring(2)], 9, dn_dev))
    far_up[1].wait_recv()
    near_up.append(relayed(ring(2), ring(1), relay_up.at[1], got_up.at[ring(2)], 4, up_dev))

    ag_up[2].wait_recv()
    ag_up[3].wait_recv()
    ag_up[5].wait_recv()
    ag_dn[2].wait_recv()
    ag_dn[3].wait_recv()
    ag_dn[4].wait_recv()
    ag_dn[5].wait_recv()
    mix[...] += dot(tok[ring(1)], w[ring(1)])

    arrive(lows)
    total = low_all[0] + low_all[1] + low_all[2] + low_all[3]
    low_t = total[0:RANK].astype(BF16)
    back_t = total[RANK:].astype(BF16)

    down_term = 2.0 * dot(back_t, tok[y])
    up_term = 2.0 * dot(low_t, ups[...])
    for t in range(CHIPS):
        source = down_term if t % 4 < 2 else up_term
        lanes = (t // 4) * LANE
        g1[t] = source[(t % 2) * TILE:(t % 2 + 1) * TILE, lanes:lanes + LANE]
    first = spread(3, g1, lambda i: h1.at[core, i], h1.at[core])

    flat = total.T
    low = flat[:, 0:RANK].astype(BF16)
    back = flat[:, RANK:].astype(BF16)
    part[y] = part[y] + 2.0 * dot(back, down_here)
    send[y] = part[y].astype(BF16)
    far_dn.append(rows_send(y, ring(2), relay_dn.at[1], 7, dn_dev))
    near_up.append(rows_send(y, ring(1), got_up.at[y], 5, up_dev))
    near_dn.append(rows_send(y, ring(3), got_dn.at[y], 10, dn_dev))
    mix[...] += 2.0 * dot(low, up_here) + dot(tok[ring(3)], w[ring(3)])

    first.wait()
    swap = push(h1.at[core], h1.at[core], ph_s.at[4], ph_r.at[4], sibling)
    owned = dot(back_a[...], h1[core].reshape(out_rows, LANE).astype(BF16))
    swap.wait_recv()
    owned += dot(back_b[...], h1[other].reshape(out_rows, LANE).astype(BF16))
    g3[...] = owned.reshape(CHIPS, TILE, LANE)
    second = spread(5, g3, lambda i: h3.at[i], h3)

    far_dn[1].wait_recv()
    near_dn.append(relayed(ring(1), ring(3), relay_dn.at[1], got_dn.at[ring(1)], 11, dn_dev))
    mixed_out[...] = (mix[...] + dot(tok[ring(2)], w[ring(2)])).astype(BF16)

    drain(0, s1)
    drain(2, s3)
    drain(3, g1)
    arrive(near_up)
    arrive(near_dn)
    for c in range(RING):
        grad_out[:, c * cols:(c + 1) * cols] = (
            part[c, here(y), :] + got_up[c].astype(F32) + got_dn[c].astype(F32)
        ).astype(BF16)
    for copy in sent:
        copy.wait_send()

    second.wait()
    for t in range(CHIPS):
        target = down_out if t % 4 < 2 else up_out
        lanes = (t // 4) * LANE
        target[0, (t % 2) * TILE:(t % 2 + 1) * TILE, lanes:lanes + LANE] = h3[t]
    drain(5, g3)


def per_device(tokens, weight, down, up, upstream, adapter, owner):
    rows, width = tokens.shape
    block, cols = upstream.shape
    any_spec = pl.BlockSpec(memory_space=pl.ANY)
    dma = lambda *shape: pltpu.SemaphoreType.DMA(shape)
    tiles = lambda *lead: pltpu.VMEM((*lead, CHIPS, TILE, LANE), F32)
    scratch = [
        pltpu.VMEM((RING, cols, cols), BF16),
        pltpu.VMEM((RING, block, cols), BF16),
        pltpu.VMEM((block, cols), BF16),
        pltpu.VMEM((RING, block, cols), F32),
        pltpu.VMEM((RING, block, cols), BF16),
        pltpu.VMEM((2, rows, cols), BF16),
        pltpu.VMEM((2, rows, cols), BF16),
        pltpu.VMEM((RING, rows, cols), BF16),
        pltpu.VMEM((RING, rows, cols), BF16),
        pltpu.VMEM((block, cols), F32),
        pltpu.VMEM((ITEM, cols), BF16),
        pltpu.VMEM((CHIPS, TAGGED, LANE), BF16),
        pltpu.VMEM((2, CHIPS, TAGGED, LANE), BF16),
        tiles(), tiles(), tiles(), tiles(2), tiles(), tiles(),
        pltpu.VMEM((RING, ITEM, block), F32),
        pltpu.VMEM((CHIPS * TILE, CHIPS * TILE), BF16),
        pltpu.VMEM((CHIPS * TILE, CHIPS * TILE), BF16),
        dma(11), dma(12), dma(12), dma(12), dma(12), dma(3), dma(3), dma(6), dma(6),
    ]
    return pl.pallas_call(
        kernel,
        out_shape=(
            pltpu.VMEM((block, cols), BF16),
            pltpu.VMEM((rows, width), BF16),
            pltpu.VMEM(down.shape, F32),
            pltpu.VMEM(up.shape, F32),
        ),
        in_specs=[any_spec] * 5
        + [pl.BlockSpec(memory_space=pltpu.SMEM), pl.BlockSpec(memory_space=pltpu.VMEM)],
        out_specs=(pl.BlockSpec(memory_space=pltpu.VMEM),) * 4,
        scratch_shapes=scratch,
        compiler_params=pltpu.CompilerParams(
            collective_id=0, has_side_effects=True, vmem_limit_bytes=63000 * 1024
        ),
        cost_estimate=pl.CostEstimate(
            flops=4 * block * width * cols, bytes_accessed=12 * 1024 * 1024, transcendentals=0
        ),
    )(tokens, weight, down, up, upstream, adapter, owner.reshape(1, -1))


def solution(mesh):
    return jax.shard_map(
        per_device,
        mesh=mesh,
        in_specs=(
            P(("dp", "tensor"), None),
            P(None, "tensor"),
            P("dp", None, "tensor"),
            P("dp", None, "tensor"),
            P("dp", "tensor"),
            P("dp", None),
            P(),
        ),
        out_specs=(
            P("dp", "tensor"),
            P(("dp", "tensor"), None),
            P("dp", None, "tensor"),
            P("dp", None, "tensor"),
        ),
        check_vma=False,
    )
```

time: 61.1 us -> 48.4 us (0.79)
  Pallas kernels: 53.3 us -> 44.3 us
  local copies, waits for them, and re-layouts: 6.28 us -> 2.67 us
    pallas_call x1, Pallas kernels: 53.3 us -> 44.3 us  [per_device(): pl.pallas_call(kernel, out_shape=(pltpu.VMEM((block, cols), BF16), pltpu....]
    unnamed x4, local copies, waits for them, and re-layouts: 6.28 us -> 2.67 us
where the time goes in v2:
time: 48.4 us; the launch traced here: 48.3 us
  Pallas kernels  44.3 us (92%)
  local copies, waits for them, and re-layouts  2.67 us (6%)
  between operations  1.29 us (3%)
    pallas_call x1, Pallas kernels, per_device(): pl.pallas_call(kernel, out_shape=(pltpu.VMEM((block, cols), BF16), pltpu....  44.3 us
    unnamed x4, local copies, waits for them, and re-layouts  2.67 us

profile of v2, /device:TPU:1, one launch (start us, length us, event | category | flops | bytes accessed | tf_op | source)
XLA Modules:
  0.0 48.3 jit_solution(1957842829991482315)
XLA Ops:
  1.3 44.3 %shard_map.102 = (bf16[128,1024]{1,0:T(8,128)(2,1)S(1)}, bf16[32,4096]{1,0:T(8,128)(2,1)S(1)}, f32[1,16,1024]{2,1,0:T(8,128)S(1)}, f32[1,16,1024]{2,1,0:T(8,128)S(1)}) custom-call(bf16[32,4096]{1,0:T(8,128)(2,1)} %tokens.1, bf16[4096,1024]{1,0:T(8,128)(2,1)} %weight.1, bf16[1,16,1024]{2,1,0:T(8,128)(2,1)} %down.1, bf16[1,16,1024]{2,1,0:T(8,128)(2,1)} %up.1, ...), custom_call_target="tpu_custom_call" | custom-call | flops 2147483648 | bytes 12582912 | tf_op jit(solution)/shard_map/pallas_call | solution.py:355
  45.6 0.7 %copy.15 = bf16[128,1024]{1,0:T(8,128)(2,1)} copy(bf16[128,1024]{1,0:T(8,128)(2,1)S(1)} %get-tuple-element.4) | data formatting | bytes 524288
  46.3 0.6 %copy.17 = f32[1,16,1024]{2,1,0:T(8,128)} copy(f32[1,16,1024]{2,1,0:T(8,128)S(1)} %get-tuple-element.6) | data formatting | bytes 131072
  47.0 0.6 %copy.18 = f32[1,16,1024]{2,1,0:T(8,128)} copy(f32[1,16,1024]{2,1,0:T(8,128)S(1)} %get-tuple-element.7) | data formatting | bytes 131072
  47.6 0.7 %copy.16 = bf16[32,4096]{1,0:T(8,128)(2,1)} copy(bf16[32,4096]{1,0:T(8,128)(2,1)S(1)} %get-tuple-element.5) | data formatting | bytes 524288

commit v3 on v2

v3 whole, which is shorter than its diff:
```python
import jax
import jax.numpy as jnp
from jax import lax
from jax.experimental import pallas as pl
from jax.experimental.pallas import tpu as pltpu
from jax.sharding import PartitionSpec as P

MESH = pl.DeviceIdType.MESH
DEEP = 8
WIDE = 4
CHIPS = DEEP * WIDE
RING = 4
RANK = 16
ITEM = 2 * RANK
LANE = 128
MIDS = 16
HALF = MIDS // 2
PIECES = [(dz, dx) for dz in (0, 2, 1, 3) for dx in (2, 1, 3, 0)]
FAR_FIRST = [
    (dz, dx) for dz in (4, 3, 5, 2, 6, 1, 7, 0) for dx in (2, 1, 3, 0) if dz or dx
]

F32 = jnp.float32
BF16 = jnp.bfloat16


def dot(a, b):
    return jnp.dot(a, b, preferred_element_type=F32)


def dot_t(a, b):
    return lax.dot_general(a, b, (((1,), (1,)), ((), ())), preferred_element_type=F32)


def one_hot(condition):
    return condition.astype(F32).astype(BF16)


def ids(rows, cols, dim):
    return lax.broadcasted_iota(jnp.int32, (rows, cols), dim)


def kernel(
    tokens, weight, down, up, upstream, adapter, owner,
    mixed_out, grad_out, down_out, up_out,
    w, tok, ups, part, send, relay_up, relay_dn, got_up, got_dn, mix,
    item, tag, tags, r1, s3, r3, g1, h1, g3, h3, low_all, back_a, back_b, block_id, owner_row,
    local_sem, ag_s, ag_r, rs_s, rs_r, low_s, low_r, ph_s, ph_r, ready,
):
    dp = lax.axis_index("dp")
    y = lax.axis_index("tensor")
    chip, core = dp // 2, dp % 2
    other = 1 - core
    is_mid = chip < MIDS
    z, x = chip // WIDE, chip % WIDE
    z_at = [lax.rem(z + j, DEEP) for j in range(DEEP)]
    x_at = [lax.rem(x + j, WIDE) for j in range(WIDE)]
    rows = tokens.shape[0]
    cols = weight.shape[1]
    ring_at = [lax.rem(y + j, RING) for j in range(RING)]
    sibling = (chip * 2 + other, y)

    def ring(step):
        return ring_at[step]

    def here(c):
        return pl.ds(pl.multiple_of(c * rows, rows), rows)

    def wide(c):
        return pl.ds(pl.multiple_of(c * cols, cols), cols)

    sent = []

    def push(src, dst, ssem, rsem, device):
        copy = pltpu.make_async_remote_copy(
            src_ref=src, dst_ref=dst, send_sem=ssem, recv_sem=rsem,
            device_id=device, device_id_type=MESH,
        )
        copy.start()
        sent.append(copy)
        return copy

    load_items = [
        pltpu.make_async_copy(down.at[0], item.at[pl.ds(0, RANK)], local_sem.at[0]),
        pltpu.make_async_copy(up.at[0], item.at[pl.ds(RANK, RANK)], local_sem.at[1]),
    ]
    order = (2, 1, 3, 0)
    load_tok = [
        pltpu.make_async_copy(
            tokens.at[:, wide(ring(k))], tok.at[ring(k), here(y)], local_sem.at[2 + k]
        )
        for k in range(RING)
    ]
    load_ups = pltpu.make_async_copy(upstream, ups, local_sem.at[6])
    load_w = [
        pltpu.make_async_copy(weight.at[wide(ring(k))], w.at[ring(k)], local_sem.at[7 + k])
        for k in range(RING)
    ]
    load_ids = [
        pltpu.make_async_copy(adapter, block_id, local_sem.at[11]),
        pltpu.make_async_copy(owner, owner_row, local_sem.at[12]),
    ]

    barrier = pltpu.get_barrier_semaphore()

    def chip_at(dz, dx):
        return z_at[dz] * WIDE + x_at[dx]

    @pl.when(is_mid)
    def _():
        for dz, dx in FAR_FIRST:
            device = (chip_at(dz, dx) * 2 + core, y)
            pl.semaphore_signal(barrier, inc=1, device_id=device, device_id_type=MESH)

    for device in [(dp, ring(k)) for k in (2, 1, 3)] + [sibling]:
        pl.semaphore_signal(barrier, inc=1, device_id=device, device_id_type=MESH)
    for copy in load_items + load_ids:
        copy.start()
    for k in order:
        load_tok[k].start()
    load_ups.start()
    for k in (2, 3, 1, 0):
        load_w[k].start()
    for copy in load_items + load_ids:
        copy.wait()
    tag[...] = jnp.broadcast_to(block_id[...].astype(F32), (1, LANE))
    for k in order:
        load_tok[k].wait()

    pl.semaphore_wait(barrier, jnp.where(is_mid, MIDS - 1, MIDS) + RING)

    up_dev, dn_dev = (dp, ring(1)), (dp, ring(3))

    def push_to(src, dst, phase, device):
        pltpu.make_async_remote_copy(
            src_ref=src, dst_ref=dst, send_sem=ph_s.at[phase], recv_sem=ph_r.at[phase],
            device_id=device, device_id_type=MESH,
        ).start()

    def piece(src, u):
        return src.at[
            pl.ds(pl.multiple_of(u // HALF * RANK, RANK), RANK),
            pl.ds(pl.multiple_of(u % HALF * LANE, LANE), LANE),
        ]

    def gather(phase, src, dst):
        for dz, dx in PIECES:
            u = lax.rem(z + dz, MIDS // WIDE) * WIDE + x_at[dx]
            if dz or dx:
                push_to(piece(src, u), dst.at[core, chip], phase, (u * 2 + core, y))
            else:
                @pl.when(is_mid)
                def _():
                    pltpu.make_async_copy(piece(src, u), dst.at[core, chip], ph_r.at[phase]).start()

                @pl.when(jnp.logical_not(is_mid))
                def _():
                    push_to(piece(src, u), dst.at[core, chip], phase, (u * 2 + core, y))

    def drain_gather(phase, like):
        @pl.when(is_mid)
        def _():
            part_of = like.at[pl.ds(0, MIDS - 1)]
            pltpu.make_async_copy(part_of, part_of, ph_s.at[phase]).wait()

        @pl.when(jnp.logical_not(is_mid))
        def _():
            part_of = like.at[pl.ds(0, MIDS)]
            pltpu.make_async_copy(part_of, part_of, ph_s.at[phase]).wait()

    def spread(phase, src, dst):
        for dz, dx in FAR_FIRST:
            to = chip_at(dz, dx)
            push_to(src.at[to], dst.at[chip], phase, (to * 2 + core, y))
        pltpu.make_async_copy(src.at[chip], dst.at[chip], ph_r.at[phase]).start()

    def drain_spread(phase, src):
        others = src.at[pl.ds(0, CHIPS - 1)]
        pltpu.make_async_copy(others, others, ph_s.at[phase]).wait()

    def landed(phase, dst):
        pltpu.make_async_copy(dst, dst, ph_r.at[phase]).wait()

    def swap(phase, both):
        copy = pltpu.make_async_remote_copy(
            src_ref=both.at[core], dst_ref=both.at[core], send_sem=ph_s.at[phase],
            recv_sem=ph_r.at[phase], device_id=sibling, device_id_type=MESH,
        )
        copy.start()
        return copy

    def arrive(copies):
        for copy in copies:
            copy.wait_recv()

    def token_send(c, owner_y, index, device):
        return push(tok.at[c, here(owner_y)], tok.at[c, here(owner_y)], ag_s.at[index], ag_r.at[index], device)

    gather(0, item, r1)
    for dz, dx in PIECES:
        u = lax.rem(z + dz, MIDS // WIDE) * WIDE + x_at[dx]
        if dz or dx:
            push_to(tag, tags.at[core, chip], 1, (u * 2 + core, y))
        else:
            @pl.when(is_mid)
            def _():
                pltpu.make_async_copy(tag, tags.at[core, chip], ph_r.at[1]).start()

            @pl.when(jnp.logical_not(is_mid))
            def _():
                push_to(tag, tags.at[core, chip], 1, (u * 2 + core, y))
    ag_up = [token_send(ring(2), y, 0, up_dev)]
    ag_dn = [token_send(ring(3), y, 6, dn_dev)]
    ag_up.append(token_send(ring(1), y, 1, up_dev))
    ag_dn.append(token_send(ring(0), y, 7, dn_dev))
    ag_up.append(token_send(ring(3), y, 2, up_dev))
    ag_dn.append(token_send(ring(2), y, 8, dn_dev))
    ag_up.append(token_send(ring(0), y, 3, up_dev))
    ag_dn.append(token_send(ring(1), y, 9, dn_dev))

    def backward(k):
        c = ring(k)
        load_w[k].wait()
        if k == 2:
            load_ups.wait()
        part[c] = dot_t(ups[...], w[c])
        if k:
            send[c] = part[c].astype(BF16)

    @pl.when(jnp.logical_not(is_mid))
    def _():
        for u in range(MIDS):
            pl.semaphore_signal(ready, inc=1, device_id=(u * 2 + core, y), device_id_type=MESH)

    adapters = owner_row.shape[1]
    span = CHIPS * RANK
    same = (ids(span, span, 0) & (RANK - 1)) == (ids(span, span, 1) & (RANK - 1))

    def users(which):
        found = jnp.broadcast_to(tags[which], (CHIPS, RANK, LANE)).reshape(span, LANE)
        return one_hot(found[:, 0:adapters].astype(jnp.int32) == ids(span, adapters, 1))

    def owners(which):
        return one_hot(owner_row[...] == (ids(span, adapters, 0) >> 4) * 2 + which)

    def matched(a, b):
        return jnp.where(same, dot_t(a, b), 0.0).astype(BF16)

    def flat(pieces):
        return pieces.reshape(span, LANE)

    backward(2)
    backward(3)

    @pl.when(is_mid)
    def _():
        landed(0, r1.at[core])
        trade = swap(2, r1)
        landed(1, tags.at[core])
        trade_tags = swap(3, tags)
        asks = users(core)
        chosen = dot(matched(asks, owners(core)), flat(r1[core]))
        take_b = matched(asks, owners(other))
        pl.semaphore_wait(ready, CHIPS - MIDS)
        trade.wait_recv()
        s3[...] = (chosen + dot(take_b, flat(r1[other]))).astype(BF16).reshape(CHIPS, RANK, LANE)
        spread(4, s3, r3)
        slots = owners(core)
        back_a[...] = matched(slots, users(core))
        trade_tags.wait_recv()
        back_b[...] = matched(slots, users(other))
        trade.wait_send()
        trade_tags.wait_send()

    ag_up[0].wait_recv()
    ag_up.append(token_send(ring(1), ring(3), 4, up_dev))
    ag_dn[0].wait_recv()
    ag_dn.append(token_send(ring(0), ring(1), 10, dn_dev))
    ag_up[1].wait_recv()
    ag_up.append(token_send(ring(0), ring(3), 5, up_dev))
    ag_dn[1].wait_recv()
    ag_dn.append(token_send(ring(1), ring(1), 11, dn_dev))

    backward(1)

    def rows_send(c, to, dst, index, device):
        return push(send.at[c, here(to)], dst, rs_s.at[index], rs_r.at[index], device)

    far_up = [
        rows_send(ring(2), ring(2), relay_up.at[0], 0, up_dev),
        rows_send(ring(3), ring(2), relay_up.at[1], 1, up_dev),
    ]
    far_dn = [rows_send(ring(1), ring(2), relay_dn.at[0], 6, dn_dev)]
    near_up = [rows_send(ring(3), ring(1), got_up.at[ring(3)], 2, up_dev)]
    near_dn = [rows_send(ring(3), ring(3), got_dn.at[ring(3)], 8, dn_dev)]

    backward(0)
    ag_up[4].wait_recv()
    mix[...] = dot(tok[y], w[y])

    landed(4, r3)
    down_here = jnp.concatenate([r3[u] for u in range(HALF)], axis=1)
    up_here = jnp.concatenate([r3[HALF + u] for u in range(HALF)], axis=1)
    low_all[y, RANK:, :] = dot_t(up_here, ups[...])
    low_all[y, 0:RANK, :] = dot_t(down_here, tok[y])
    lows = [
        push(low_all.at[y], low_all.at[y], low_s.at[k - 1], low_r.at[k - 1], (dp, ring(k)))
        for k in (2, 1, 3)
    ]

    def relayed(c, to, relay, dst, index, device):
        send[c, here(to), :] = (part[c, here(to), :] + relay[...].astype(F32)).astype(BF16)
        return rows_send(c, to, dst, index, device)

    far_up[0].wait_recv()
    near_up.append(relayed(ring(1), ring(1), relay_up.at[0], got_up.at[ring(1)], 3, up_dev))
    far_dn[0].wait_recv()
    near_dn.append(relayed(ring(2), ring(3), relay_dn.at[0], got_dn.at[ring(2)], 9, dn_dev))
    far_up[1].wait_recv()
    near_up.append(relayed(ring(2), ring(1), relay_up.at[1], got_up.at[ring(2)], 4, up_dev))

    ag_up[2].wait_recv()
    ag_up[3].wait_recv()
    ag_up[5].wait_recv()
    ag_dn[2].wait_recv()
    ag_dn[3].wait_recv()
    ag_dn[4].wait_recv()
    ag_dn[5].wait_recv()
    mix[...] += dot(tok[ring(1)], w[ring(1)])

    arrive(lows)
    total = low_all[0] + low_all[1] + low_all[2] + low_all[3]
    low_t = total[0:RANK].astype(BF16)
    back_t = total[RANK:].astype(BF16)

    g1[0:RANK, :] = (2.0 * dot(back_t, tok[y])).astype(BF16)
    g1[RANK:, :] = (2.0 * dot(low_t, ups[...])).astype(BF16)
    gather(5, g1, h1)

    turned = total.T
    low = turned[:, 0:RANK].astype(BF16)
    back = turned[:, RANK:].astype(BF16)
    part[y] = part[y] + 2.0 * dot(back, down_here)
    send[y] = part[y].astype(BF16)
    far_dn.append(rows_send(y, ring(2), relay_dn.at[1], 7, dn_dev))
    near_up.append(rows_send(y, ring(1), got_up.at[y], 5, up_dev))
    near_dn.append(rows_send(y, ring(3), got_dn.at[y], 10, dn_dev))
    mix[...] += 2.0 * dot(low, up_here) + dot(tok[ring(3)], w[ring(3)])

    @pl.when(is_mid)
    def _():
        landed(5, h1.at[core])
        trade = swap(6, h1)
        owned = dot(back_a[...], flat(h1[core]))
        trade.wait_recv()
        owned += dot(back_b[...], flat(h1[other]))
        g3[...] = owned.astype(BF16).reshape(CHIPS, RANK, LANE)
        spread(7, g3, h3)
        trade.wait_send()

    far_dn[1].wait_recv()
    near_dn.append(relayed(ring(1), ring(3), relay_dn.at[1], got_dn.at[ring(1)], 11, dn_dev))
    mixed_out[...] = (mix[...] + dot(tok[ring(2)], w[ring(2)])).astype(BF16)

    drain_gather(0, r3)
    drain_gather(1, tags.at[core])
    drain_gather(5, r3)
    arrive(near_up)
    arrive(near_dn)
    for c in range(RING):
        grad_out[:, c * cols:(c + 1) * cols] = (
            part[c, here(y), :] + got_up[c].astype(F32) + got_dn[c].astype(F32)
        ).astype(BF16)
    for copy in sent:
        copy.wait_send()

    landed(7, h3)
    for u in range(HALF):
        lanes = slice(u * LANE, (u + 1) * LANE)
        down_out[0, :, lanes] = h3[u].astype(F32)
        up_out[0, :, lanes] = h3[HALF + u].astype(F32)

    @pl.when(is_mid)
    def _():
        drain_spread(4, s3)
        drain_spread(7, g3)


def per_device(tokens, weight, down, up, upstream, adapter, owner):
    rows, width = tokens.shape
    block, cols = upstream.shape
    any_spec = pl.BlockSpec(memory_space=pl.ANY)
    dma = lambda *shape: pltpu.SemaphoreType.DMA(shape)
    pieces = lambda *lead: pltpu.VMEM((*lead, RANK, LANE), BF16)
    scratch = [
        pltpu.VMEM((RING, cols, cols), BF16),
        pltpu.VMEM((RING, block, cols), BF16),
        pltpu.VMEM((block, cols), BF16),
        pltpu.VMEM((RING, block, cols), F32),
        pltpu.VMEM((RING, block, cols), BF16),
        pltpu.VMEM((2, rows, cols), BF16),
        pltpu.VMEM((2, rows, cols), BF16),
        pltpu.VMEM((RING, rows, cols), BF16),
        pltpu.VMEM((RING, rows, cols), BF16),
        pltpu.VMEM((block, cols), F32),
        pltpu.VMEM((ITEM, cols), BF16),
        pltpu.VMEM((1, LANE), F32),
        pltpu.VMEM((2, CHIPS, 1, LANE), F32),
        pieces(2, CHIPS), pieces(CHIPS), pieces(MIDS),
        pltpu.VMEM((ITEM, cols), BF16),
        pieces(2, CHIPS), pieces(CHIPS), pieces(MIDS),
        pltpu.VMEM((RING, ITEM, block), F32),
        pltpu.VMEM((CHIPS * RANK, CHIPS * RANK), BF16),
        pltpu.VMEM((CHIPS * RANK, CHIPS * RANK), BF16),
        pltpu.VMEM(adapter.shape, jnp.int32),
        pltpu.VMEM((1, owner.shape[0]), jnp.int32),
        dma(13), dma(12), dma(12), dma(12), dma(12), dma(3), dma(3), dma(8), dma(8),
        pltpu.SemaphoreType.REGULAR,
    ]
    return pl.pallas_call(
        kernel,
        out_shape=(
            pltpu.VMEM((block, cols), BF16),
            pltpu.VMEM((rows, width), BF16),
            pltpu.VMEM(down.shape, F32),
            pltpu.VMEM(up.shape, F32),
        ),
        in_specs=[any_spec] * 5 + [pl.BlockSpec(memory_space=pltpu.HBM), any_spec],
        out_specs=(pl.BlockSpec(memory_space=pltpu.VMEM),) * 4,
        scratch_shapes=scratch,
        compiler_params=pltpu.CompilerParams(
            collective_id=0, has_side_effects=True, vmem_limit_bytes=63000 * 1024
        ),
        cost_estimate=pl.CostEstimate(
            flops=4 * block * width * cols, bytes_accessed=12 * 1024 * 1024, transcendentals=0
        ),
    )(tokens, weight, down, up, upstream, adapter, owner.reshape(1, -1))


def solution(mesh):
    return jax.shard_map(
        per_device,
        mesh=mesh,
        in_specs=(
            P(("dp", "tensor"), None),
            P(None, "tensor"),
            P("dp", None, "tensor"),
            P("dp", None, "tensor"),
            P("dp", "tensor"),
            P("dp", None),
            P(),
        ),
        out_specs=(
            P("dp", "tensor"),
            P(("dp", "tensor"), None),
            P("dp", None, "tensor"),
            P("dp", None, "tensor"),
        ),
        check_vma=False,
    )
```

time: 48.4 us -> 47.1 us (0.973)
  Pallas kernels: 44.3 us -> 43.1 us
    pallas_call x1, Pallas kernels: 44.3 us -> 43.1 us  [per_device(): pl.pallas_call(kernel, out_shape=(pltpu.VMEM((block, cols), BF16), pltpu....]
where the time goes in v3:
time: 47.1 us; the launch traced here: 47 us
  Pallas kernels  43.1 us (92%)
  local copies, waits for them, and re-layouts  2.67 us (6%)
  between operations  1.29 us (3%)
    pallas_call x1, Pallas kernels, per_device(): pl.pallas_call(kernel, out_shape=(pltpu.VMEM((block, cols), BF16), pltpu....  43.1 us
    unnamed x4, local copies, waits for them, and re-layouts  2.67 us

profile of v3, /device:TPU:1, one launch (start us, length us, event | category | flops | bytes accessed | tf_op | source)
XLA Modules:
  0.0 47.0 jit_solution(1177812741966172949)
XLA Ops:
  1.3 43.1 %shard_map.102 = (bf16[128,1024]{1,0:T(8,128)(2,1)S(1)}, bf16[32,4096]{1,0:T(8,128)(2,1)S(1)}, f32[1,16,1024]{2,1,0:T(8,128)S(1)}, f32[1,16,1024]{2,1,0:T(8,128)S(1)}) custom-call(bf16[32,4096]{1,0:T(8,128)(2,1)} %tokens.1, bf16[4096,1024]{1,0:T(8,128)(2,1)} %weight.1, bf16[1,16,1024]{2,1,0:T(8,128)(2,1)} %down.1, bf16[1,16,1024]{2,1,0:T(8,128)(2,1)} %up.1, ...), custom_call_target="tpu_custom_call" | custom-call | flops 2147483648 | bytes 12582912 | tf_op jit(solution)/shard_map/pallas_call | solution.py:420
  44.3 0.7 %copy.15 = bf16[128,1024]{1,0:T(8,128)(2,1)} copy(bf16[128,1024]{1,0:T(8,128)(2,1)S(1)} %get-tuple-element.4) | data formatting | bytes 524288
  45.1 0.6 %copy.17 = f32[1,16,1024]{2,1,0:T(8,128)} copy(f32[1,16,1024]{2,1,0:T(8,128)S(1)} %get-tuple-element.6) | data formatting | bytes 131072
  45.7 0.6 %copy.18 = f32[1,16,1024]{2,1,0:T(8,128)} copy(f32[1,16,1024]{2,1,0:T(8,128)S(1)} %get-tuple-element.7) | data formatting | bytes 131072
  46.3 0.7 %copy.16 = bf16[32,4096]{1,0:T(8,128)(2,1)} copy(bf16[32,4096]{1,0:T(8,128)(2,1)S(1)} %get-tuple-element.5) | data formatting | bytes 524288

commit v4 on v3

--- a/solution.py
+++ b/solution.py
@@ -13,11 +13,13 @@
 RANK = 16
 ITEM = 2 * RANK
 LANE = 128
-MIDS = 16
-HALF = MIDS // 2
-PIECES = [(dz, dx) for dz in (0, 2, 1, 3) for dx in (2, 1, 3, 0)]
-FAR_FIRST = [
-    (dz, dx) for dz in (4, 3, 5, 2, 6, 1, 7, 0) for dx in (2, 1, 3, 0) if dz or dx
+CORES = 2 * CHIPS
+MIDS = CORES // 2
+EIGHT = 8
+SPAN = CORES * EIGHT
+PIECES = [(dz, dx, dc) for dz in (4, 6, 2, 0) for dx in (2, 1, 3, 0) for dc in (0, 1)]
+EVERY = [
+    (dz, dx, dc) for dz in (4, 3, 5, 2, 6, 1, 7, 0) for dx in (2, 1, 3, 0) for dc in (0, 1)
 ]
 
 F32 = jnp.float32
@@ -44,21 +46,22 @@
     tokens, weight, down, up, upstream, adapter, owner,
     mixed_out, grad_out, down_out, up_out,
     w, tok, ups, part, send, relay_up, relay_dn, got_up, got_dn, mix,
-    item, tag, tags, r1, s3, r3, g1, h1, g3, h3, low_all, back_a, back_b, block_id, owner_row,
+    item, tag, tags, s1, r1, s3, r3, g1, h1, g3, h3, low_all, back, block_id, owner_row,
     local_sem, ag_s, ag_r, rs_s, rs_r, low_s, low_r, ph_s, ph_r, ready,
 ):
     dp = lax.axis_index("dp")
     y = lax.axis_index("tensor")
     chip, core = dp // 2, dp % 2
-    other = 1 - core
-    is_mid = chip < MIDS
     z, x = chip // WIDE, chip % WIDE
+    is_mid = z % 2 == 0
+    mine = z // 2 * (2 * WIDE) + x * 2 + core
     z_at = [lax.rem(z + j, DEEP) for j in range(DEEP)]
     x_at = [lax.rem(x + j, WIDE) for j in range(WIDE)]
     rows = tokens.shape[0]
     cols = weight.shape[1]
     ring_at = [lax.rem(y + j, RING) for j in range(RING)]
-    sibling = (chip * 2 + other, y)
+    z_mid = [lax.rem(z // 2 + j, DEEP // 2) for j in range(DEEP // 2)]
+    cores = [core, 1 - core]
 
     def ring(step):
         return ring_at[step]
@@ -103,17 +106,17 @@
 
     barrier = pltpu.get_barrier_semaphore()
 
-    def chip_at(dz, dx):
-        return z_at[dz] * WIDE + x_at[dx]
+    def at(dz, dx, dc):
+        return z_at[dz] * (2 * WIDE) + x_at[dx] * 2 + cores[dc]
 
     @pl.when(is_mid)
     def _():
-        for dz, dx in FAR_FIRST:
-            device = (chip_at(dz, dx) * 2 + core, y)
-            pl.semaphore_signal(barrier, inc=1, device_id=device, device_id_type=MESH)
-
-    for device in [(dp, ring(k)) for k in (2, 1, 3)] + [sibling]:
-        pl.semaphore_signal(barrier, inc=1, device_id=device, device_id_type=MESH)
+        for step in EVERY:
+            if any(step):
+                pl.semaphore_signal(barrier, inc=1, device_id=(at(*step), y), device_id_type=MESH)
+
+    for k in (2, 1, 3):
+        pl.semaphore_signal(barrier, inc=1, device_id=(dp, ring(k)), device_id_type=MESH)
     for copy in load_items + load_ids:
         copy.start()
     for k in order:
@@ -124,10 +127,15 @@
     for copy in load_items + load_ids:
         copy.wait()
     tag[...] = jnp.broadcast_to(block_id[...].astype(F32), (1, LANE))
+    for v in range(MIDS):
+        lanes = (v // 4) * LANE
+        if v % 2 == 0:
+            pair = item[v % 4 * EIGHT:v % 4 * EIGHT + RANK, lanes:lanes + LANE].astype(F32)
+        s1[v] = pair[(v % 2) * EIGHT:(v % 2 + 1) * EIGHT].astype(BF16)
     for k in order:
         load_tok[k].wait()
 
-    pl.semaphore_wait(barrier, jnp.where(is_mid, MIDS - 1, MIDS) + RING)
+    pl.semaphore_wait(barrier, jnp.where(is_mid, MIDS - 1, MIDS) + RING - 1)
 
     up_dev, dn_dev = (dp, ring(1)), (dp, ring(3))
 
@@ -137,25 +145,24 @@
             device_id=device, device_id_type=MESH,
         ).start()
 
-    def piece(src, u):
-        return src.at[
-            pl.ds(pl.multiple_of(u // HALF * RANK, RANK), RANK),
-            pl.ds(pl.multiple_of(u % HALF * LANE, LANE), LANE),
-        ]
-
-    def gather(phase, src, dst):
-        for dz, dx in PIECES:
-            u = lax.rem(z + dz, MIDS // WIDE) * WIDE + x_at[dx]
-            if dz or dx:
-                push_to(piece(src, u), dst.at[core, chip], phase, (u * 2 + core, y))
+    def gather(pairs):
+        for dz, dx, dc in PIECES:
+            mid = z_mid[dz // 2] * (2 * WIDE) + x_at[dx] * 2 + cores[dc]
+            to = z_mid[dz // 2] * (4 * WIDE) + x_at[dx] * 2 + cores[dc]
+
+            def move():
+                for phase, src, dst in pairs:
+                    push_to(src(mid), dst.at[dp], phase, (to, y))
+
+            if dz or dx or dc:
+                move()
             else:
                 @pl.when(is_mid)
                 def _():
-                    pltpu.make_async_copy(piece(src, u), dst.at[core, chip], ph_r.at[phase]).start()
-
-                @pl.when(jnp.logical_not(is_mid))
-                def _():
-                    push_to(piece(src, u), dst.at[core, chip], phase, (u * 2 + core, y))
+                    for phase, src, dst in pairs:
+                        pltpu.make_async_copy(src(mid), dst.at[dp], ph_r.at[phase]).start()
+
+                pl.when(jnp.logical_not(is_mid))(move)
 
     def drain_gather(phase, like):
         @pl.when(is_mid)
@@ -169,25 +176,19 @@
             pltpu.make_async_copy(part_of, part_of, ph_s.at[phase]).wait()
 
     def spread(phase, src, dst):
-        for dz, dx in FAR_FIRST:
-            to = chip_at(dz, dx)
-            push_to(src.at[to], dst.at[chip], phase, (to * 2 + core, y))
-        pltpu.make_async_copy(src.at[chip], dst.at[chip], ph_r.at[phase]).start()
+        for step in EVERY:
+            to = at(*step)
+            if any(step):
+                push_to(src.at[to], dst.at[mine], phase, (to, y))
+            else:
+                pltpu.make_async_copy(src.at[dp], dst.at[mine], ph_r.at[phase]).start()
 
     def drain_spread(phase, src):
-        others = src.at[pl.ds(0, CHIPS - 1)]
+        others = src.at[pl.ds(0, CORES - 1)]
         pltpu.make_async_copy(others, others, ph_s.at[phase]).wait()
 
     def landed(phase, dst):
         pltpu.make_async_copy(dst, dst, ph_r.at[phase]).wait()
-
-    def swap(phase, both):
-        copy = pltpu.make_async_remote_copy(
-            src_ref=both.at[core], dst_ref=both.at[core], send_sem=ph_s.at[phase],
-            recv_sem=ph_r.at[phase], device_id=sibling, device_id_type=MESH,
-        )
-        copy.start()
-        return copy
 
     def arrive(copies):
         for copy in copies:
@@ -196,19 +197,7 @@
     def token_send(c, owner_y, index, device):
         return push(tok.at[c, here(owner_y)], tok.at[c, here(owner_y)], ag_s.at[index], ag_r.at[index], device)
 
-    gather(0, item, r1)
-    for dz, dx in PIECES:
-        u = lax.rem(z + dz, MIDS // WIDE) * WIDE + x_at[dx]
-        if dz or dx:
-            push_to(tag, tags.at[core, chip], 1, (u * 2 + core, y))
-        else:
-            @pl.when(is_mid)
-            def _():
-                pltpu.make_async_copy(tag, tags.at[core, chip], ph_r.at[1]).start()
-
-            @pl.when(jnp.logical_not(is_mid))
-            def _():
-                push_to(tag, tags.at[core, chip], 1, (u * 2 + core, y))
+    gather([(0, lambda v: s1.at[v], r1), (1, lambda v: tag, tags)])
     ag_up = [token_send(ring(2), y, 0, up_dev)]
     ag_dn = [token_send(ring(3), y, 6, dn_dev)]
     ag_up.append(token_send(ring(1), y, 1, up_dev))
@@ -229,48 +218,38 @@
 
     @pl.when(jnp.logical_not(is_mid))
     def _():
-        for u in range(MIDS):
-            pl.semaphore_signal(ready, inc=1, device_id=(u * 2 + core, y), device_id_type=MESH)
+        for dz, dx, dc in PIECES:
+            to = z_mid[dz // 2] * (4 * WIDE) + x_at[dx] * 2 + cores[dc]
+            pl.semaphore_signal(ready, inc=1, device_id=(to, y), device_id_type=MESH)
 
     adapters = owner_row.shape[1]
-    span = CHIPS * RANK
-    same = (ids(span, span, 0) & (RANK - 1)) == (ids(span, span, 1) & (RANK - 1))
-
-    def users(which):
-        found = jnp.broadcast_to(tags[which], (CHIPS, RANK, LANE)).reshape(span, LANE)
-        return one_hot(found[:, 0:adapters].astype(jnp.int32) == ids(span, adapters, 1))
-
-    def owners(which):
-        return one_hot(owner_row[...] == (ids(span, adapters, 0) >> 4) * 2 + which)
+    same = (ids(SPAN, SPAN, 0) & (EIGHT - 1)) == (ids(SPAN, SPAN, 1) & (EIGHT - 1))
+
+    def users():
+        found = jnp.broadcast_to(tags[...], (CORES, EIGHT, LANE)).reshape(SPAN, LANE)
+        return one_hot(found[:, 0:adapters].astype(jnp.int32) == ids(SPAN, adapters, 1))
+
+    def owners():
+        return one_hot(owner_row[...] == ids(SPAN, adapters, 0) >> 3)
 
     def matched(a, b):
         return jnp.where(same, dot_t(a, b), 0.0).astype(BF16)
 
     def flat(pieces):
-        return pieces.reshape(span, LANE)
+        return pieces[...].astype(F32).reshape(SPAN, LANE).astype(BF16)
 
     backward(2)
     backward(3)
 
     @pl.when(is_mid)
     def _():
-        landed(0, r1.at[core])
-        trade = swap(2, r1)
-        landed(1, tags.at[core])
-        trade_tags = swap(3, tags)
-        asks = users(core)
-        chosen = dot(matched(asks, owners(core)), flat(r1[core]))
-        take_b = matched(asks, owners(other))
-        pl.semaphore_wait(ready, CHIPS - MIDS)
-        trade.wait_recv()
-        s3[...] = (chosen + dot(take_b, flat(r1[other]))).astype(BF16).reshape(CHIPS, RANK, LANE)
+        landed(1, tags)
+        take = matched(users(), owners())
+        landed(0, r1)
+        pl.semaphore_wait(ready, CORES - MIDS)
+        s3[...] = dot(take, flat(r1)).reshape(CORES, EIGHT, LANE).astype(BF16)
         spread(4, s3, r3)
-        slots = owners(core)
-        back_a[...] = matched(slots, users(core))
-        trade_tags.wait_recv()
-        back_b[...] = matched(slots, users(other))
-        trade.wait_send()
-        trade_tags.wait_send()
+        back[...] = matched(owners(), users())
 
     ag_up[0].wait_recv()
     ag_up.append(token_send(ring(1), ring(3), 4, up_dev))
@@ -299,8 +278,17 @@
     mix[...] = dot(tok[y], w[y])
 
     landed(4, r3)
-    down_here = jnp.concatenate([r3[u] for u in range(HALF)], axis=1)
-    up_here = jnp.concatenate([r3[HALF + u] for u in range(HALF)], axis=1)
+
+    def half_item(base):
+        return jnp.concatenate(
+            [
+                jnp.concatenate([r3[v].astype(F32), r3[v + 1].astype(F32)], axis=0)
+                for v in range(base, MIDS, 4)
+            ],
+            axis=1,
+        ).astype(BF16)
+
+    down_here, up_here = half_item(0), half_item(2)
     low_all[y, RANK:, :] = dot_t(up_here, ups[...])
     low_all[y, 0:RANK, :] = dot_t(down_here, tok[y])
     lows = [
@@ -333,14 +321,18 @@
     low_t = total[0:RANK].astype(BF16)
     back_t = total[RANK:].astype(BF16)
 
-    g1[0:RANK, :] = (2.0 * dot(back_t, tok[y])).astype(BF16)
-    g1[RANK:, :] = (2.0 * dot(low_t, ups[...])).astype(BF16)
-    gather(5, g1, h1)
+    down_term = 2.0 * dot(back_t, tok[y])
+    up_term = 2.0 * dot(low_t, ups[...])
+    for v in range(MIDS):
+        source = down_term if v % 4 < 2 else up_term
+        lanes = (v // 4) * LANE
+        g1[v] = source[(v % 2) * EIGHT:(v % 2 + 1) * EIGHT, lanes:lanes + LANE].astype(BF16)
+    gather([(5, lambda v: g1.at[v], h1)])
 
     turned = total.T
     low = turned[:, 0:RANK].astype(BF16)
-    back = turned[:, RANK:].astype(BF16)
-    part[y] = part[y] + 2.0 * dot(back, down_here)
+    low_back = turned[:, RANK:].astype(BF16)
+    part[y] = part[y] + 2.0 * dot(low_back, down_here)
     send[y] = part[y].astype(BF16)
     far_dn.append(rows_send(y, ring(2), relay_dn.at[1], 7, dn_dev))
     near_up.append(rows_send(y, ring(1), got_up.at[y], 5, up_dev))
@@ -349,21 +341,16 @@
 
     @pl.when(is_mid)
     def _():
-        landed(5, h1.at[core])
-        trade = swap(6, h1)
-        owned = dot(back_a[...], flat(h1[core]))
-        trade.wait_recv()
-        owned += dot(back_b[...], flat(h1[other]))
-        g3[...] = owned.astype(BF16).reshape(CHIPS, RANK, LANE)
+        landed(5, h1)
+        g3[...] = dot(back[...], flat(h1)).reshape(CORES, EIGHT, LANE).astype(BF16)
         spread(7, g3, h3)
-        trade.wait_send()
 
     far_dn[1].wait_recv()
     near_dn.append(relayed(ring(1), ring(3), relay_dn.at[1], got_dn.at[ring(1)], 11, dn_dev))
     mixed_out[...] = (mix[...] + dot(tok[ring(2)], w[ring(2)])).astype(BF16)
 
     drain_gather(0, r3)
-    drain_gather(1, tags.at[core])
+    drain_gather(1, tags)
     drain_gather(5, r3)
     arrive(near_up)
     arrive(near_dn)
@@ -375,10 +362,10 @@
         copy.wait_send()
 
     landed(7, h3)
-    for u in range(HALF):
-        lanes = slice(u * LANE, (u + 1) * LANE)
-        down_out[0, :, lanes] = h3[u].astype(F32)
-        up_out[0, :, lanes] = h3[HALF + u].astype(F32)
+    for v in range(MIDS):
+        target = down_out if v % 4 < 2 else up_out
+        lanes = (v // 4) * LANE
+        target[0, (v % 2) * EIGHT:(v % 2 + 1) * EIGHT, lanes:lanes + LANE] = h3[v].astype(F32)
 
     @pl.when(is_mid)
     def _():
@@ -391,7 +378,7 @@
     block, cols = upstream.shape
     any_spec = pl.BlockSpec(memory_space=pl.ANY)
     dma = lambda *shape: pltpu.SemaphoreType.DMA(shape)
-    pieces = lambda *lead: pltpu.VMEM((*lead, RANK, LANE), BF16)
+    pieces = lambda n: pltpu.VMEM((n, EIGHT, LANE), BF16)
     scratch = [
         pltpu.VMEM((RING, cols, cols), BF16),
         pltpu.VMEM((RING, block, cols), BF16),
@@ -405,13 +392,11 @@
         pltpu.VMEM((block, cols), F32),
         pltpu.VMEM((ITEM, cols), BF16),
         pltpu.VMEM((1, LANE), F32),
-        pltpu.VMEM((2, CHIPS, 1, LANE), F32),
-        pieces(2, CHIPS), pieces(CHIPS), pieces(MIDS),
-        pltpu.VMEM((ITEM, cols), BF16),
-        pieces(2, CHIPS), pieces(CHIPS), pieces(MIDS),
+        pltpu.VMEM((CORES, 1, LANE), F32),
+        pieces(MIDS), pieces(CORES), pieces(CORES), pieces(MIDS),
+        pieces(MIDS), pieces(CORES), pieces(CORES), pieces(MIDS),
         pltpu.VMEM((RING, ITEM, block), F32),
-        pltpu.VMEM((CHIPS * RANK, CHIPS * RANK), BF16),
-        pltpu.VMEM((CHIPS * RANK, CHIPS * RANK), BF16),
+        pltpu.VMEM((SPAN, SPAN), BF16),
         pltpu.VMEM(adapter.shape, jnp.int32),
         pltpu.VMEM((1, owner.shape[0]), jnp.int32),
         dma(13), dma(12), dma(12), dma(12), dma(12), dma(3), dma(3), dma(8), dma(8),

time: 47.1 us -> 47.3 us (level)
  no operation moved by 1% of the time
where the time goes in v4:
time: 47.3 us
  Pallas kernels  43.3 us (92%)
  local copies, waits for them, and re-layouts  2.67 us (6%)
  between operations  1.29 us (3%)
    pallas_call x1, Pallas kernels, per_device(): pl.pallas_call(kernel, out_shape=(pltpu.VMEM((block, cols), BF16), pltpu....  43.3 us
    unnamed x4, local copies, waits for them, and re-layouts  2.67 us

profile of v4, /device:TPU:1, one launch (start us, length us, event | category | flops | bytes accessed | tf_op | source)
XLA Modules:
  0.0 47.3 jit_solution(9999873374796111117)
XLA Ops:
  1.3 43.3 %shard_map.102 = (bf16[128,1024]{1,0:T(8,128)(2,1)S(1)}, bf16[32,4096]{1,0:T(8,128)(2,1)S(1)}, f32[1,16,1024]{2,1,0:T(8,128)S(1)}, f32[1,16,1024]{2,1,0:T(8,128)S(1)}) custom-call(bf16[32,4096]{1,0:T(8,128)(2,1)} %tokens.1, bf16[4096,1024]{1,0:T(8,128)(2,1)} %weight.1, bf16[1,16,1024]{2,1,0:T(8,128)(2,1)} %down.1, bf16[1,16,1024]{2,1,0:T(8,128)(2,1)} %up.1, ...), custom_call_target="tpu_custom_call" | custom-call | flops 2147483648 | bytes 12582912 | tf_op jit(solution)/shard_map/pallas_call | solution.py:405
  44.6 0.7 %copy.15 = bf16[128,1024]{1,0:T(8,128)(2,1)} copy(bf16[128,1024]{1,0:T(8,128)(2,1)S(1)} %get-tuple-element.4) | data formatting | bytes 524288
  45.3 0.6 %copy.17 = f32[1,16,1024]{2,1,0:T(8,128)} copy(f32[1,16,1024]{2,1,0:T(8,128)S(1)} %get-tuple-element.6) | data formatting | bytes 131072
  45.9 0.6 %copy.18 = f32[1,16,1024]{2,1,0:T(8,128)} copy(f32[1,16,1024]{2,1,0:T(8,128)S(1)} %get-tuple-element.7) | data formatting | bytes 131072
  46.5 0.7 %copy.16 = bf16[32,4096]{1,0:T(8,128)(2,1)} copy(bf16[32,4096]{1,0:T(8,128)(2,1)S(1)} %get-tuple-element.5) | data formatting | bytes 524288

commit v5 on v4

--- a/solution.py
+++ b/solution.py
@@ -46,21 +46,24 @@
     tokens, weight, down, up, upstream, adapter, owner,
     mixed_out, grad_out, down_out, up_out,
     w, tok, ups, part, send, relay_up, relay_dn, got_up, got_dn, mix,
-    item, tag, tags, s1, r1, s3, r3, g1, h1, g3, h3, low_all, back, block_id, owner_row,
-    local_sem, ag_s, ag_r, rs_s, rs_r, low_s, low_r, ph_s, ph_r, ready,
+    item, tag, tags, s1, r1, s3, r3, g1, h1, g3, h3, low_all, tags_back, block_id, owner_row,
+    local_sem, ag_s, ag_r, rs_s, rs_r, low_s, low_r, ph_s, ph_r,
 ):
     dp = lax.axis_index("dp")
     y = lax.axis_index("tensor")
     chip, core = dp // 2, dp % 2
     z, x = chip // WIDE, chip % WIDE
-    is_mid = z % 2 == 0
-    mine = z // 2 * (2 * WIDE) + x * 2 + core
+    half_deep = DEEP // 2
+    mid_there, mid_back = z < half_deep, z % 2 == 0
+    spot_there = z * (2 * WIDE) + x * 2 + core
+    spot_back = z // 2 * (2 * WIDE) + x * 2 + core
     z_at = [lax.rem(z + j, DEEP) for j in range(DEEP)]
     x_at = [lax.rem(x + j, WIDE) for j in range(WIDE)]
     rows = tokens.shape[0]
     cols = weight.shape[1]
     ring_at = [lax.rem(y + j, RING) for j in range(RING)]
-    z_mid = [lax.rem(z // 2 + j, DEEP // 2) for j in range(DEEP // 2)]
+    z_there = [lax.rem(z + j, half_deep) for j in range(half_deep)]
+    z_back = [lax.rem(z // 2 + j, half_deep) for j in range(half_deep)]
     cores = [core, 1 - core]
 
     def ring(step):
@@ -109,7 +112,7 @@
     def at(dz, dx, dc):
         return z_at[dz] * (2 * WIDE) + x_at[dx] * 2 + cores[dc]
 
-    @pl.when(is_mid)
+    @pl.when(mid_there)
     def _():
         for step in EVERY:
             if any(step):
@@ -126,7 +129,10 @@
         load_w[k].start()
     for copy in load_items + load_ids:
         copy.wait()
-    tag[...] = jnp.broadcast_to(block_id[...].astype(F32), (1, LANE))
+    adapters = owner_row.shape[1]
+    hit = ids(1, adapters, 1) == block_id[...]
+    slot = jnp.sum(jnp.where(hit, owner_row[...].astype(F32), 0.0), axis=1, keepdims=True)
+    tag[...] = jnp.broadcast_to(slot, (1, LANE))
     for v in range(MIDS):
         lanes = (v // 4) * LANE
         if v % 2 == 0:
@@ -135,7 +141,7 @@
     for k in order:
         load_tok[k].wait()
 
-    pl.semaphore_wait(barrier, jnp.where(is_mid, MIDS - 1, MIDS) + RING - 1)
+    pl.semaphore_wait(barrier, jnp.where(mid_there, MIDS - 1, MIDS) + RING - 1)
 
     up_dev, dn_dev = (dp, ring(1)), (dp, ring(3))
 
@@ -145,10 +151,10 @@
             device_id=device, device_id_type=MESH,
         ).start()
 
-    def gather(pairs):
+    def gather(pairs, z_mid, stride, is_mid):
         for dz, dx, dc in PIECES:
-            mid = z_mid[dz // 2] * (2 * WIDE) + x_at[dx] * 2 + cores[dc]
-            to = z_mid[dz // 2] * (4 * WIDE) + x_at[dx] * 2 + cores[dc]
+            plane, rest = z_mid[dz // 2], x_at[dx] * 2 + cores[dc]
+            mid, to = plane * (2 * WIDE) + rest, plane * (stride * 2 * WIDE) + rest
 
             def move():
                 for phase, src, dst in pairs:
@@ -164,7 +170,7 @@
 
                 pl.when(jnp.logical_not(is_mid))(move)
 
-    def drain_gather(phase, like):
+    def drain_gather(phase, like, is_mid):
         @pl.when(is_mid)
         def _():
             part_of = like.at[pl.ds(0, MIDS - 1)]
@@ -175,7 +181,7 @@
             part_of = like.at[pl.ds(0, MIDS)]
             pltpu.make_async_copy(part_of, part_of, ph_s.at[phase]).wait()
 
-    def spread(phase, src, dst):
+    def spread(phase, src, dst, mine):
         for step in EVERY:
             to = at(*step)
             if any(step):
@@ -197,7 +203,7 @@
     def token_send(c, owner_y, index, device):
         return push(tok.at[c, here(owner_y)], tok.at[c, here(owner_y)], ag_s.at[index], ag_r.at[index], device)
 
-    gather([(0, lambda v: s1.at[v], r1), (1, lambda v: tag, tags)])
+    gather([(0, lambda v: s1.at[v], r1), (1, lambda v: tag, tags)], z_there, 1, mid_there)
     ag_up = [token_send(ring(2), y, 0, up_dev)]
     ag_dn = [token_send(ring(3), y, 6, dn_dev)]
     ag_up.append(token_send(ring(1), y, 1, up_dev))
@@ -216,24 +222,19 @@
         if k:
             send[c] = part[c].astype(BF16)
 
-    @pl.when(jnp.logical_not(is_mid))
-    def _():
-        for dz, dx, dc in PIECES:
-            to = z_mid[dz // 2] * (4 * WIDE) + x_at[dx] * 2 + cores[dc]
-            pl.semaphore_signal(ready, inc=1, device_id=(to, y), device_id_type=MESH)
-
-    adapters = owner_row.shape[1]
-    same = (ids(SPAN, SPAN, 0) & (EIGHT - 1)) == (ids(SPAN, SPAN, 1) & (EIGHT - 1))
-
-    def users():
-        found = jnp.broadcast_to(tags[...], (CORES, EIGHT, LANE)).reshape(SPAN, LANE)
-        return one_hot(found[:, 0:adapters].astype(jnp.int32) == ids(SPAN, adapters, 1))
-
-    def owners():
-        return one_hot(owner_row[...] == ids(SPAN, adapters, 0) >> 3)
-
-    def matched(a, b):
-        return jnp.where(same, dot_t(a, b), 0.0).astype(BF16)
+    def slot_rows(tags):
+        return jnp.broadcast_to(tags[...], (CORES, EIGHT, LANE)).reshape(SPAN, LANE).astype(jnp.int32)
+
+    def taking(tags):
+        wanted = slot_rows(tags) * EIGHT + (ids(SPAN, LANE, 0) & (EIGHT - 1))
+        wanted = jnp.concatenate([wanted] * (SPAN // LANE), axis=1)
+        return one_hot(wanted == ids(SPAN, SPAN, 1))
+
+    def giving(tags):
+        has = one_hot(slot_rows(tags)[:, 0:CORES] == ids(SPAN, CORES, 1))
+        slots = one_hot(ids(SPAN, CORES, 0) >> 3 == ids(SPAN, CORES, 1))
+        same = (ids(SPAN, SPAN, 0) & (EIGHT - 1)) == (ids(SPAN, SPAN, 1) & (EIGHT - 1))
+        return jnp.where(same, dot_t(slots, has), 0.0).astype(BF16)
 
     def flat(pieces):
         return pieces[...].astype(F32).reshape(SPAN, LANE).astype(BF16)
@@ -241,15 +242,13 @@
     backward(2)
     backward(3)
 
-    @pl.when(is_mid)
+    @pl.when(mid_there)
     def _():
         landed(1, tags)
-        take = matched(users(), owners())
+        take = taking(tags)
         landed(0, r1)
-        pl.semaphore_wait(ready, CORES - MIDS)
         s3[...] = dot(take, flat(r1)).reshape(CORES, EIGHT, LANE).astype(BF16)
-        spread(4, s3, r3)
-        back[...] = matched(owners(), users())
+        spread(4, s3, r3, spot_there)
 
     ag_up[0].wait_recv()
     ag_up.append(token_send(ring(1), ring(3), 4, up_dev))
@@ -296,16 +295,11 @@
         for k in (2, 1, 3)
     ]
 
+    gather([(2, lambda v: tag, tags_back)], z_back, 2, mid_back)
+
     def relayed(c, to, relay, dst, index, device):
         send[c, here(to), :] = (part[c, here(to), :] + relay[...].astype(F32)).astype(BF16)
         return rows_send(c, to, dst, index, device)
-
-    far_up[0].wait_recv()
-    near_up.append(relayed(ring(1), ring(1), relay_up.at[0], got_up.at[ring(1)], 3, up_dev))
-    far_dn[0].wait_recv()
-    near_dn.append(relayed(ring(2), ring(3), relay_dn.at[0], got_dn.at[ring(2)], 9, dn_dev))
-    far_up[1].wait_recv()
-    near_up.append(relayed(ring(2), ring(1), relay_up.at[1], got_up.at[ring(2)], 4, up_dev))
 
     ag_up[2].wait_recv()
     ag_up[3].wait_recv()
@@ -327,7 +321,7 @@
         source = down_term if v % 4 < 2 else up_term
         lanes = (v // 4) * LANE
         g1[v] = source[(v % 2) * EIGHT:(v % 2 + 1) * EIGHT, lanes:lanes + LANE].astype(BF16)
-    gather([(5, lambda v: g1.at[v], h1)])
+    gather([(5, lambda v: g1.at[v], h1)], z_back, 2, mid_back)
 
     turned = total.T
     low = turned[:, 0:RANK].astype(BF16)
@@ -337,21 +331,32 @@
     far_dn.append(rows_send(y, ring(2), relay_dn.at[1], 7, dn_dev))
     near_up.append(rows_send(y, ring(1), got_up.at[y], 5, up_dev))
     near_dn.append(rows_send(y, ring(3), got_dn.at[y], 10, dn_dev))
+    far_up[0].wait_recv()
+    near_up.append(relayed(ring(1), ring(1), relay_up.at[0], got_up.at[ring(1)], 3, up_dev))
+    far_dn[0].wait_recv()
+    near_dn.append(relayed(ring(2), ring(3), relay_dn.at[0], got_dn.at[ring(2)], 9, dn_dev))
+    far_up[1].wait_recv()
+    near_up.append(relayed(ring(2), ring(1), relay_up.at[1], got_up.at[ring(2)], 4, up_dev))
+
     mix[...] += 2.0 * dot(low, up_here) + dot(tok[ring(3)], w[ring(3)])
-
-    @pl.when(is_mid)
-    def _():
-        landed(5, h1)
-        g3[...] = dot(back[...], flat(h1)).reshape(CORES, EIGHT, LANE).astype(BF16)
-        spread(7, g3, h3)
 
     far_dn[1].wait_recv()
     near_dn.append(relayed(ring(1), ring(3), relay_dn.at[1], got_dn.at[ring(1)], 11, dn_dev))
+
+    @pl.when(mid_back)
+    def _():
+        landed(2, tags_back)
+        give = giving(tags_back)
+        landed(5, h1)
+        g3[...] = dot(give, flat(h1)).reshape(CORES, EIGHT, LANE).astype(BF16)
+        spread(7, g3, h3, spot_back)
+
     mixed_out[...] = (mix[...] + dot(tok[ring(2)], w[ring(2)])).astype(BF16)
 
-    drain_gather(0, r3)
-    drain_gather(1, tags)
-    drain_gather(5, r3)
+    drain_gather(0, r3, mid_there)
+    drain_gather(1, tags, mid_there)
+    drain_gather(2, tags, mid_back)
+    drain_gather(5, r3, mid_back)
     arrive(near_up)
     arrive(near_dn)
     for c in range(RING):
@@ -367,9 +372,12 @@
         lanes = (v // 4) * LANE
         target[0, (v % 2) * EIGHT:(v % 2 + 1) * EIGHT, lanes:lanes + LANE] = h3[v].astype(F32)
 
-    @pl.when(is_mid)
+    @pl.when(mid_there)
     def _():
         drain_spread(4, s3)
+
+    @pl.when(mid_back)
+    def _():
         drain_spread(7, g3)
 
 
@@ -396,11 +404,10 @@
         pieces(MIDS), pieces(CORES), pieces(CORES), pieces(MIDS),
         pieces(MIDS), pieces(CORES), pieces(CORES), pieces(MIDS),
         pltpu.VMEM((RING, ITEM, block), F32),
-        pltpu.VMEM((SPAN, SPAN), BF16),
+        pltpu.VMEM((CORES, 1, LANE), F32),
         pltpu.VMEM(adapter.shape, jnp.int32),
         pltpu.VMEM((1, owner.shape[0]), jnp.int32),
         dma(13), dma(12), dma(12), dma(12), dma(12), dma(3), dma(3), dma(8), dma(8),
-        pltpu.SemaphoreType.REGULAR,
     ]
     return pl.pallas_call(
         kernel,

time: 47.3 us -> 46.5 us (0.983)
  Pallas kernels: 43.3 us -> 42.4 us
    pallas_call x1, Pallas kernels: 43.3 us -> 42.4 us  [per_device(): pl.pallas_call(kernel, out_shape=(pltpu.VMEM((block, cols), BF16), pltpu....]
where the time goes in v5:
time: 46.5 us; the launch traced here: 46.4 us
  Pallas kernels  42.4 us (91%)
  local copies, waits for them, and re-layouts  2.67 us (6%)
  between operations  1.29 us (3%)
    pallas_call x1, Pallas kernels, per_device(): pl.pallas_call(kernel, out_shape=(pltpu.VMEM((block, cols), BF16), pltpu....  42.4 us
    unnamed x4, local copies, waits for them, and re-layouts  2.67 us

profile of v5, /device:TPU:1, one launch (start us, length us, event | category | flops | bytes accessed | tf_op | source)
XLA Modules:
  0.0 46.4 jit_solution(10275505248020789185)
XLA Ops:
  1.3 42.4 %shard_map.102 = (bf16[128,1024]{1,0:T(8,128)(2,1)S(1)}, bf16[32,4096]{1,0:T(8,128)(2,1)S(1)}, f32[1,16,1024]{2,1,0:T(8,128)S(1)}, f32[1,16,1024]{2,1,0:T(8,128)S(1)}) custom-call(bf16[32,4096]{1,0:T(8,128)(2,1)} %tokens.1, bf16[4096,1024]{1,0:T(8,128)(2,1)} %weight.1, bf16[1,16,1024]{2,1,0:T(8,128)(2,1)} %down.1, bf16[1,16,1024]{2,1,0:T(8,128)(2,1)} %up.1, ...), custom_call_target="tpu_custom_call" | custom-call | flops 2147483648 | bytes 12582912 | tf_op jit(solution)/shard_map/pallas_call | solution.py:412
  43.7 0.7 %copy.15 = bf16[128,1024]{1,0:T(8,128)(2,1)} copy(bf16[128,1024]{1,0:T(8,128)(2,1)S(1)} %get-tuple-element.4) | data formatting | bytes 524288
  44.4 0.6 %copy.17 = f32[1,16,1024]{2,1,0:T(8,128)} copy(f32[1,16,1024]{2,1,0:T(8,128)S(1)} %get-tuple-element.6) | data formatting | bytes 131072
  45.0 0.6 %copy.18 = f32[1,16,1024]{2,1,0:T(8,128)} copy(f32[1,16,1024]{2,1,0:T(8,128)S(1)} %get-tuple-element.7) | data formatting | bytes 131072
  45.7 0.7 %copy.16 = bf16[32,4096]{1,0:T(8,128)(2,1)} copy(bf16[32,4096]{1,0:T(8,128)(2,1)S(1)} %get-tuple-element.5) | data formatting | bytes 524288

commit v6 on v5

--- a/solution.py
+++ b/solution.py
@@ -44,7 +44,7 @@
 
 def kernel(
     tokens, weight, down, up, upstream, adapter, owner,
-    mixed_out, grad_out, down_out, up_out,
+    mixed_out, grad_out, pair_out,
     w, tok, ups, part, send, relay_up, relay_dn, got_up, got_dn, mix,
     item, tag, tags, s1, r1, s3, r3, g1, h1, g3, h3, low_all, tags_back, block_id, owner_row,
     local_sem, ag_s, ag_r, rs_s, rs_r, low_s, low_r, ph_s, ph_r,
@@ -264,14 +264,6 @@
     def rows_send(c, to, dst, index, device):
         return push(send.at[c, here(to)], dst, rs_s.at[index], rs_r.at[index], device)
 
-    far_up = [
-        rows_send(ring(2), ring(2), relay_up.at[0], 0, up_dev),
-        rows_send(ring(3), ring(2), relay_up.at[1], 1, up_dev),
-    ]
-    far_dn = [rows_send(ring(1), ring(2), relay_dn.at[0], 6, dn_dev)]
-    near_up = [rows_send(ring(3), ring(1), got_up.at[ring(3)], 2, up_dev)]
-    near_dn = [rows_send(ring(3), ring(3), got_dn.at[ring(3)], 8, dn_dev)]
-
     backward(0)
     ag_up[4].wait_recv()
     mix[...] = dot(tok[y], w[y])
@@ -296,6 +288,14 @@
     ]
 
     gather([(2, lambda v: tag, tags_back)], z_back, 2, mid_back)
+
+    far_up = [
+        rows_send(ring(2), ring(2), relay_up.at[0], 0, up_dev),
+        rows_send(ring(3), ring(2), relay_up.at[1], 1, up_dev),
+    ]
+    far_dn = [rows_send(ring(1), ring(2), relay_dn.at[0], 6, dn_dev)]
+    near_up = [rows_send(ring(3), ring(1), got_up.at[ring(3)], 2, up_dev)]
+    near_dn = [rows_send(ring(3), ring(3), got_dn.at[ring(3)], 8, dn_dev)]
 
     def relayed(c, to, relay, dst, index, device):
         send[c, here(to), :] = (part[c, here(to), :] + relay[...].astype(F32)).astype(BF16)
@@ -367,10 +367,10 @@
         copy.wait_send()
 
     landed(7, h3)
-    for v in range(MIDS):
-        target = down_out if v % 4 < 2 else up_out
+    for v in range(0, MIDS, 2):
         lanes = (v // 4) * LANE
-        target[0, (v % 2) * EIGHT:(v % 2 + 1) * EIGHT, lanes:lanes + LANE] = h3[v].astype(F32)
+        rows_16 = jnp.concatenate([h3[v].astype(F32), h3[v + 1].astype(F32)], axis=0)
+        pair_out[v % 4 // 2, :, lanes:lanes + LANE] = rows_16.astype(BF16)
 
     @pl.when(mid_there)
     def _():
@@ -409,16 +409,15 @@
         pltpu.VMEM((1, owner.shape[0]), jnp.int32),
         dma(13), dma(12), dma(12), dma(12), dma(12), dma(3), dma(3), dma(8), dma(8),
     ]
-    return pl.pallas_call(
+    mixed, grad, pair = pl.pallas_call(
         kernel,
         out_shape=(
             pltpu.VMEM((block, cols), BF16),
             pltpu.VMEM((rows, width), BF16),
-            pltpu.VMEM(down.shape, F32),
-            pltpu.VMEM(up.shape, F32),
+            pltpu.VMEM((2, RANK, cols), BF16),
         ),
         in_specs=[any_spec] * 5 + [pl.BlockSpec(memory_space=pltpu.HBM), any_spec],
-        out_specs=(pl.BlockSpec(memory_space=pltpu.VMEM),) * 4,
+        out_specs=(pl.BlockSpec(memory_space=pltpu.VMEM),) * 3,
         scratch_shapes=scratch,
         compiler_params=pltpu.CompilerParams(
             collective_id=0, has_side_effects=True, vmem_limit_bytes=63000 * 1024
@@ -427,6 +426,8 @@
             flops=4 * block * width * cols, bytes_accessed=12 * 1024 * 1024, transcendentals=0
         ),
     )(tokens, weight, down, up, upstream, adapter, owner.reshape(1, -1))
+    pair = pair.astype(F32)
+    return mixed, grad, pair[:1], pair[1:]
 
 
 def solution(mesh):

time: 46.5 us -> 44.6 us (0.959)
  Pallas kernels: 42.4 us -> 41.1 us
  local copies, waits for them, and re-layouts: 2.67 us -> 2.06 us
    pallas_call x1, Pallas kernels: 42.4 us -> 41.1 us  [per_device(): pl.pallas_call(kernel, out_shape=(pltpu.VMEM((block, cols), BF16), pltpu....]
    unnamed x4 -> x2, local copies, waits for them, and re-layouts: 2.67 us -> 1.41 us
    slice x0 -> x1, local copies, waits for them, and re-layouts: none -> 0.66 us  [per_device(): return (mixed, grad, pair[:1], pair[1:])]
where the time goes in v6:
time: 44.6 us; the launch traced here: 44.5 us
  Pallas kernels  41.1 us (92%)
  local copies, waits for them, and re-layouts  2.06 us (5%)
  between operations  1.29 us (3%)
    pallas_call x1, Pallas kernels, per_device(): pl.pallas_call(kernel, out_shape=(pltpu.VMEM((block, cols), BF16), pltpu....  41.1 us
    unnamed x2, local copies, waits for them, and re-layouts  1.41 us

profile of v6, /device:TPU:1, one launch (start us, length us, event | category | flops | bytes accessed | tf_op | source)
XLA Modules:
  0.0 44.5 jit_solution(13058647002678610767)
XLA Ops:
  1.3 41.1 %shard_map.102 = (bf16[128,1024]{1,0:T(8,128)(2,1)S(1)}, bf16[32,4096]{1,0:T(8,128)(2,1)S(1)}, bf16[2,16,1024]{2,1,0:T(8,128)(2,1)S(1)}) custom-call(bf16[32,4096]{1,0:T(8,128)(2,1)} %tokens.1, bf16[4096,1024]{1,0:T(8,128)(2,1)} %weight.1, bf16[1,16,1024]{2,1,0:T(8,128)(2,1)} %down.1, bf16[1,16,1024]{2,1,0:T(8,128)(2,1)} %up.1, bf16[128,1024]{1,0:T(8,128)(2,1)} %upstream.1, ...), custom_call_target="tpu_custom_call" | custom-call | flops 2147483648 | bytes 12582912 | tf_op jit(solution)/shard_map/pallas_call | solution.py:412
  42.4 0.7 %copy.13 = bf16[128,1024]{1,0:T(8,128)(2,1)} copy(bf16[128,1024]{1,0:T(8,128)(2,1)S(1)} %get-tuple-element.12) | data formatting | bytes 524288
  43.1 0.7 %copy.14 = bf16[32,4096]{1,0:T(8,128)(2,1)} copy(bf16[32,4096]{1,0:T(8,128)(2,1)S(1)} %get-tuple-element.13) | data formatting | bytes 524288
  43.8 0.7 %fusion = (f32[1,16,1024]{2,1,0:T(8,128)}, f32[1,16,1024]{2,1,0:T(8,128)}) fusion(bf16[2,16,1024]{2,1,0:T(8,128)(2,1)S(1)} %get-tuple-element.9), kind=kLoop, calls=%fused_computation | loop fusion | bytes 262144 | tf_op jit(solution)/shard_map/slice | solution.py:430

commit v7 on v6

--- a/solution.py
+++ b/solution.py
@@ -340,6 +340,8 @@
 
     mix[...] += 2.0 * dot(low, up_here) + dot(tok[ring(3)], w[ring(3)])
 
+    mixed_out[...] = (mix[...] + dot(tok[ring(2)], w[ring(2)])).astype(BF16)
+
     far_dn[1].wait_recv()
     near_dn.append(relayed(ring(1), ring(3), relay_dn.at[1], got_dn.at[ring(1)], 11, dn_dev))
 
@@ -351,7 +353,6 @@
         g3[...] = dot(give, flat(h1)).reshape(CORES, EIGHT, LANE).astype(BF16)
         spread(7, g3, h3, spot_back)
 
-    mixed_out[...] = (mix[...] + dot(tok[ring(2)], w[ring(2)])).astype(BF16)
 
     drain_gather(0, r3, mid_there)
     drain_gather(1, tags, mid_there)

time: 44.6 us -> 44.6 us (level)
  no operation moved by 1% of the time
where the time goes in v7:
time: 44.6 us; the launch traced here: 44.5 us
  Pallas kernels  41.1 us (92%)
  local copies, waits for them, and re-layouts  2.06 us (5%)
  between operations  1.29 us (3%)
    pallas_call x1, Pallas kernels, per_device(): pl.pallas_call(kernel, out_shape=(pltpu.VMEM((block, cols), BF16), pltpu....  41.1 us
    unnamed x2, local copies, waits for them, and re-layouts  1.41 us

profile of v7, /device:TPU:1, one launch (start us, length us, event | category | flops | bytes accessed | tf_op | source)
XLA Modules:
  0.0 44.5 jit_solution(13327767656739556986)
XLA Ops:
  1.3 41.1 %shard_map.102 = (bf16[128,1024]{1,0:T(8,128)(2,1)S(1)}, bf16[32,4096]{1,0:T(8,128)(2,1)S(1)}, bf16[2,16,1024]{2,1,0:T(8,128)(2,1)S(1)}) custom-call(bf16[32,4096]{1,0:T(8,128)(2,1)} %tokens.1, bf16[4096,1024]{1,0:T(8,128)(2,1)} %weight.1, bf16[1,16,1024]{2,1,0:T(8,128)(2,1)} %down.1, bf16[1,16,1024]{2,1,0:T(8,128)(2,1)} %up.1, bf16[128,1024]{1,0:T(8,128)(2,1)} %upstream.1, ...), custom_call_target="tpu_custom_call" | custom-call | flops 2147483648 | bytes 12582912 | tf_op jit(solution)/shard_map/pallas_call | solution.py:413
  42.4 0.7 %copy.13 = bf16[128,1024]{1,0:T(8,128)(2,1)} copy(bf16[128,1024]{1,0:T(8,128)(2,1)S(1)} %get-tuple-element.12) | data formatting | bytes 524288
  43.1 0.7 %copy.14 = bf16[32,4096]{1,0:T(8,128)(2,1)} copy(bf16[32,4096]{1,0:T(8,128)(2,1)S(1)} %get-tuple-element.13) | data formatting | bytes 524288
  43.8 0.7 %fusion = (f32[1,16,1024]{2,1,0:T(8,128)}, f32[1,16,1024]{2,1,0:T(8,128)}) fusion(bf16[2,16,1024]{2,1,0:T(8,128)(2,1)S(1)} %get-tuple-element.9), kind=kLoop, calls=%fused_computation | loop fusion | bytes 262144 | tf_op jit(solution)/shard_map/slice | solution.py:431

commit v8 on v7

--- a/solution.py
+++ b/solution.py
@@ -112,14 +112,15 @@
     def at(dz, dx, dc):
         return z_at[dz] * (2 * WIDE) + x_at[dx] * 2 + cores[dc]
 
+    for k in (2, 1, 3):
+        pl.semaphore_signal(barrier, inc=1, device_id=(dp, ring(k)), device_id_type=MESH)
+
     @pl.when(mid_there)
     def _():
         for step in EVERY:
             if any(step):
                 pl.semaphore_signal(barrier, inc=1, device_id=(at(*step), y), device_id_type=MESH)
 
-    for k in (2, 1, 3):
-        pl.semaphore_signal(barrier, inc=1, device_id=(dp, ring(k)), device_id_type=MESH)
     for copy in load_items + load_ids:
         copy.start()
     for k in order:

time: 44.6 us -> 44.6 us (level)
  no operation moved by 1% of the time
where the time goes in v8:
time: 44.6 us; the launch traced here: 44.5 us
  Pallas kernels  41.1 us (92%)
  local copies, waits for them, and re-layouts  2.06 us (5%)
  between operations  1.29 us (3%)
    pallas_call x1, Pallas kernels, per_device(): pl.pallas_call(kernel, out_shape=(pltpu.VMEM((block, cols), BF16), pltpu....  41.1 us
    unnamed x2, local copies, waits for them, and re-layouts  1.41 us

profile of v8, /device:TPU:1, one launch (start us, length us, event | category | flops | bytes accessed | tf_op | source)
XLA Modules:
  0.0 44.5 jit_solution(5142453268063437553)
XLA Ops:
  1.3 41.1 %shard_map.102 = (bf16[128,1024]{1,0:T(8,128)(2,1)S(1)}, bf16[32,4096]{1,0:T(8,128)(2,1)S(1)}, bf16[2,16,1024]{2,1,0:T(8,128)(2,1)S(1)}) custom-call(bf16[32,4096]{1,0:T(8,128)(2,1)} %tokens.1, bf16[4096,1024]{1,0:T(8,128)(2,1)} %weight.1, bf16[1,16,1024]{2,1,0:T(8,128)(2,1)} %down.1, bf16[1,16,1024]{2,1,0:T(8,128)(2,1)} %up.1, bf16[128,1024]{1,0:T(8,128)(2,1)} %upstream.1, ...), custom_call_target="tpu_custom_call" | custom-call | flops 2147483648 | bytes 12582912 | tf_op jit(solution)/shard_map/pallas_call | solution.py:414
  42.4 0.7 %copy.13 = bf16[128,1024]{1,0:T(8,128)(2,1)} copy(bf16[128,1024]{1,0:T(8,128)(2,1)S(1)} %get-tuple-element.12) | data formatting | bytes 524288
  43.1 0.7 %copy.14 = bf16[32,4096]{1,0:T(8,128)(2,1)} copy(bf16[32,4096]{1,0:T(8,128)(2,1)S(1)} %get-tuple-element.13) | data formatting | bytes 524288
  43.8 0.7 %fusion = (f32[1,16,1024]{2,1,0:T(8,128)}, f32[1,16,1024]{2,1,0:T(8,128)}) fusion(bf16[2,16,1024]{2,1,0:T(8,128)(2,1)S(1)} %get-tuple-element.9), kind=kLoop, calls=%fused_computation | loop fusion | bytes 262144 | tf_op jit(solution)/shard_map/slice | solution.py:432
